TPU v7x, 256 devices: a whole 4x4x8 slice. The times are simulated.
256 devices in a mesh: seq: 32 (over x_hi, z, core), head: 8 (over y, x_lo).
Axes of the slice: x: 4 (x_hi: 2, x_lo: 2; x = x_hi * 2 + x_lo), y: 4, z: 8, core: 2. Of those that a mesh axis runs over, the one named last changes fastest.
Arguments:
- prompt_queries: bfloat16 [4096, 1024], P('seq', 'head'), may hold values from -130 to 130
- prompt_cache: bfloat16 [4096, 256], P('seq'), may hold values from -7 to 7
- response_queries: bfloat16 [32768, 1024], P('seq', 'head'), may hold values from -130 to 130
- response_cache: bfloat16 [32768, 256], P('seq'), may hold values from -6 to 6
- prompt_cotangent: bfloat16 [4096, 1024], P('seq', 'head'), may hold values from -6 to 6
- response_cotangent: bfloat16 [32768, 1024], P('seq', 'head'), may hold values from -6 to 6
- response_lengths: int32 [32], P('seq'), may hold values from 0 to 1024, as said below
Outputs:
- prompt_output: bfloat16 [4096, 1024], P('seq', 'head')
- response_output: bfloat16 [32768, 1024], P('seq', 'head')
- prompt_adjoint: bfloat16 [4096, 1024], P('seq', 'head')
- response_adjoint: bfloat16 [32768, 1024], P('seq', 'head')
- prompt_cachegrad: bfloat16 [4096, 256], P('seq')
- response_cachegrad: bfloat16 [32768, 256], P('seq')
Inputs may be any that keep to these rules, and one draw needn't show every extreme that they name: `response_lengths`: 16 slots are non-empty; a non-empty slot holds 512 or more tokens; in every draw some slot holds 1024 tokens.
All inputs are finite; a program needn't handle non-finite values.
Results may differ from a plain program's by a relative error of at most 0.011.
Values may be sent and summed in bfloat16 or wider, within the bound.
No kernel may reach another device: no remote copies, remote signals or barrier semaphores. Data moves between devices by JAX's collectives and lax.ppermute only.
A program may use at most 128 MiB of HBM per device.

v0:
```python
import math

import jax
import jax.numpy as jnp
from jax import lax
from jax.sharding import PartitionSpec as P


def head_pass(query, keys, values, cotangent, mask, live):
    scale = 1.0 / math.sqrt(query.shape[1])
    scores = jnp.dot(query, keys.T, preferred_element_type=jnp.float32) * scale
    scores = jnp.where(mask, scores, -1e30)
    highest = jnp.max(scores, axis=1, keepdims=True)
    raised = jnp.where(mask, jnp.exp(scores - highest), 0.0)
    totals = jnp.sum(raised, axis=1, keepdims=True) + jnp.where(live, 0.0, 1.0)[:, None]
    probs = raised / totals
    rounded = probs.astype(jnp.bfloat16)
    attended = jnp.dot(rounded, values, preferred_element_type=jnp.float32)
    slopes = jnp.dot(cotangent, values.T, preferred_element_type=jnp.float32)
    offset = jnp.sum(cotangent.astype(jnp.float32) * attended, axis=1, keepdims=True)
    score_grad = (probs * (slopes - offset)).astype(jnp.bfloat16)
    query_grad = jnp.dot(score_grad, keys, preferred_element_type=jnp.float32) * scale
    key_grad = jnp.dot(score_grad.T, query, preferred_element_type=jnp.float32) * scale
    value_grad = jnp.dot(rounded.T, cotangent, preferred_element_type=jnp.float32)
    return (attended.astype(jnp.bfloat16), query_grad.astype(jnp.bfloat16), key_grad, value_grad)


def merge_heads(stacked):
    return jnp.transpose(stacked, (1, 0, 2)).reshape(stacked.shape[1], -1)


def group_pass(queries, keys, values, cotangent, mask, live):
    width = keys.shape[1]
    heads = queries.shape[1] // width

    def one_head(head):
        return head_pass(queries, keys, values, cotangent, mask, live)

    attended, query_grad, key_grad, value_grad = lax.map(
        one_head, jnp.arange(heads, dtype=jnp.int32)
    )
    return (
        merge_heads(attended),
        merge_heads(query_grad),
        jnp.sum(key_grad, axis=0),
        jnp.sum(value_grad, axis=0),
    )


def slot_pass(queries, cache, cotangent, length, prompt_keys, prompt_values):
    width = prompt_keys.shape[1]
    span = queries.shape[0]
    count = prompt_keys.shape[0]
    block = 512
    keys = jnp.concatenate([prompt_keys, cache[:, :width]], axis=0)
    values = jnp.concatenate([prompt_values, cache[:, width:]], axis=0)
    columns = jnp.arange(span, dtype=jnp.int32)
    outputs = []
    adjoints = []
    key_total = jnp.zeros((count + span, width), jnp.float32)
    value_total = jnp.zeros((count + span, width), jnp.float32)
    for begin in range(0, span, block):
        position = begin + jnp.arange(block, dtype=jnp.int32)
        live = position < length
        own = (columns[None, :] <= position[:, None]) & live[:, None]
        mask = jnp.concatenate([jnp.broadcast_to(live[:, None], (block, count)), own], axis=1)
        attended, query_grad, key_grad, value_grad = group_pass(
            queries[begin : begin + block],
            keys,
            values,
            cotangent[begin : begin + block],
            mask,
            live,
        )
        outputs.append(attended)
        adjoints.append(query_grad)
        key_total = key_total + key_grad
        value_total = value_total + value_grad
    prompt_part = jnp.concatenate([key_total[:count], value_total[:count]], axis=1)
    own_part = jnp.concatenate([key_total[count:], value_total[count:]], axis=1)
    return (
        jnp.concatenate(outputs, axis=0),
        jnp.concatenate(adjoints, axis=0),
        prompt_part,
        own_part,
    )


def maybe_slot(queries, cache, cotangent, length, prompt_keys, prompt_values):
    width = prompt_keys.shape[1]
    count = prompt_keys.shape[0]
    span = queries.shape[0]

    def busy(unused):
        return slot_pass(queries, cache, cotangent, length, prompt_keys, prompt_values)

    def empty(unused):
        return (
            jnp.zeros_like(queries),
            jnp.zeros_like(queries),
            jnp.zeros((count, 2 * width), jnp.float32),
            jnp.zeros((span, 2 * width), jnp.float32),
        )

    return lax.cond(length > 0, busy, empty, 0)


def on_device(
    prompt_queries,
    prompt_cache,
    response_queries,
    response_cache,
    prompt_cotangent,
    response_cotangent,
    response_lengths,
):
    share = prompt_cache.shape[0]
    width = prompt_cache.shape[1] // 2
    whole = lax.all_gather(prompt_cache, "seq", axis=0, tiled=True)
    prompt_keys = whole[:, :width]
    prompt_values = whole[:, width:]
    count = whole.shape[0]
    first = lax.axis_index("seq") * share
    query_rows = first + jnp.arange(share, dtype=jnp.int32)
    key_rows = jnp.arange(count, dtype=jnp.int32)
    mask = key_rows[None, :] <= query_rows[:, None]
    live = jnp.ones((share,), dtype=jnp.bool_)
    prompt_output, prompt_adjoint, key_grad, value_grad = group_pass(
        prompt_queries, prompt_keys, prompt_values, prompt_cotangent, mask, live
    )
    prompt_part = jnp.concatenate([key_grad, value_grad], axis=1)
    result = maybe_slot(
        response_queries,
        response_cache,
        response_cotangent,
        response_lengths[0],
        prompt_keys,
        prompt_values,
    )
    outputs = [result[0]]
    adjoints = [result[1]]
    prompt_part = prompt_part + result[2]
    owns = result[3]
    response_output = jnp.concatenate(outputs, axis=0)
    response_adjoint = jnp.concatenate(adjoints, axis=0)
    share_sum = lax.psum_scatter(prompt_part, "seq", scatter_dimension=0, tiled=True)
    prompt_sum = lax.psum(share_sum, "head")
    prompt_cachegrad = prompt_sum.astype(jnp.bfloat16)
    response_sum = lax.psum(owns, "head")
    response_cachegrad = response_sum.astype(jnp.bfloat16)
    return (
        prompt_output,
        response_output,
        prompt_adjoint,
        response_adjoint,
        prompt_cachegrad,
        response_cachegrad,
    )


def solution(mesh):
    return jax.shard_map(
        on_device,
        mesh=mesh,
        in_specs=(
            P("seq", "head"),
            P("seq", None),
            P("seq", "head"),
            P("seq", None),
            P("seq", "head"),
            P("seq", "head"),
            P("seq"),
        ),
        out_specs=(
            P("seq", "head"),
            P("seq", "head"),
            P("seq", "head"),
            P("seq", "head"),
            P("seq", None),
            P("seq", None),
        ),
        check_vma=False,
    )
```

profile of v0, /device:TPU:2, one launch (start us, length us, event | category | flops | bytes accessed | tf_op | source)
XLA Modules:
  0.0 375.7 jit_solution(8837716222109653356)
XLA Ops:
  9.5 83.3 %all-gather.2.cloned.1.call-done = bf16[4096,256]{1,0:T(8,128)(2,1)} async-done(((bf16[128,256]{1,0:T(8,128)(2,1)}), bf16[4096,256]{1,0:T(8,128)(2,1)}) %all-gather.2.cloned.1.call-update) | async-done | bytes 2097168 | tf_op jit(solution)/shard_map/all_gather | solution.py:119
  92.8 1.8 fusion.47
  96.0 1.8 fusion.37
  98.9 1.8 convolution_multiply_fusion.2
  101.9 58.8 %conditional.1 = (bf16[1024,128]{1,0:T(8,128)(2,1)}, bf16[1024,128]{1,0:T(8,128)(2,1)}, f32[4096,256]{0,1:T(8,128)}, f32[1024,256]{0,1:T(8,128)}) conditional(s32[]{:T(128)} %convert_element_type.71, () %tuple.22, (s32[]{:T(128)}, bf16[1024,256]{1,0:T(8,128)(2,1)S(1)}, bf16[4096,128]{1,0:T(8,128)(2,1)S(1)}, bf16[1024,128]{1,0:T(8,128)(2,1)S(1)}, ...), branch_computations={%region_2.0_spmd, %region_3.10_spmd} | conditional | flops 8191347200 | bytes 396144192 | solution.py:105
  103.7 2.0 fusion.3
  105.6 3.3 fusion.8
  110.3 2.0 fusion.2
  112.3 3.1 fusion.6
  115.4 0.9 copy-done.2
  116.9 3.1 fusion.7
  120.1 1.5 fusion.10
  121.7 2.4 copy-done.3
  124.2 3.3 fusion.5
  127.5 1.7 multiply_reduce_fusion.1
  129.9 3.8 %fusion = bf16[512,5120]{0,1:T(8,128)(2,1)} fusion(f32[512,5120]{0,1:T(8,128)S(1)} %fusion.7, f32[512]{0:T(512)S(1)} %get-tuple-element.141, bf16[1024,128]{1,0:T(8,128)(2,1)S(1)} %get-tuple-element.116, bf16[1024,128]{1,0:T(8,128)(2,1)S(1)} %get-tuple-element.144, bf16[4096,128]{1,0:T(8,128)(2,1)S(1)} %get-tuple-element.73), kind=kOutput, calls=%fused_computation.1 | convolution fusion | flops 681574400 | bytes 17172480 | tf_op jit(solution)/shard_map/cond/branch_1_fun/while/body/eval_jaxpr/dot_general | solution.py:19
  133.8 4.1 %fusion.19 = bf16[512,128]{1,0:T(8,128)(2,1)S(1)} fusion(bf16[512,5120]{0,1:T(8,128)(2,1)} %fusion, bf16[1024,128]{1,0:T(8,128)(2,1)S(1)} %copy-done.20, bf16[4096,128]{1,0:T(8,128)(2,1)S(1)} %copy-done.13), kind=kOutput, calls=%fused_computation.36 | convolution fusion | flops 673841152 | bytes 6684672 | tf_op jit(solution)/shard_map/cond/branch_1_fun/while/body/eval_jaxpr/dot_general | solution.py:22
  137.8 3.9 %fusion.1 = bf16[512,5120]{0,1:T(8,128)(2,1)} fusion(f32[512,5120]{0,1:T(8,128)S(1)} %fusion.5, f32[512]{0:T(512)S(1)} %get-tuple-element.140, bf16[1024,128]{1,0:T(8,128)(2,1)S(1)} %get-tuple-element.116, bf16[1024,128]{1,0:T(8,128)(2,1)S(1)} %get-tuple-element.144, bf16[4096,128]{1,0:T(8,128)(2,1)S(1)} %get-tuple-element.73), kind=kOutput, calls=%fused_computation.3 | convolution fusion | flops 681574400 | bytes 17172480 | tf_op jit(solution)/shard_map/cond/branch_1_fun/while/body/eval_jaxpr/dot_general | solution.py:19
  141.7 4.1 %fusion.18 = bf16[512,128]{1,0:T(8,128)(2,1)S(1)} fusion(bf16[512,5120]{0,1:T(8,128)(2,1)} %fusion.1, bf16[1024,128]{1,0:T(8,128)(2,1)S(1)} %copy-done.20, bf16[4096,128]{1,0:T(8,128)(2,1)S(1)} %copy-done.13), kind=kOutput, calls=%fused_computation.35 | convolution fusion | flops 673841152 | bytes 6684672 | tf_op jit(solution)/shard_map/cond/branch_1_fun/while/body/eval_jaxpr/dot_general | solution.py:22
  146.5 1.9 fusion.12
  148.4 1.9 convolution_add_fusion
  150.6 1.8 fusion.23
  152.4 1.1 slice-done
  153.7 1.8 fusion.4
  155.7 1.4 slice-done.4
  157.1 2.4 pad_maximum_fusion
  159.6 1.2 pad_maximum_fusion.3
  160.8 6.1 %maximum_add_fusion = f32[4096,256]{0,1:T(8,128)} fusion(f32[4096,256]{0,1:T(8,128)} %get-tuple-element.98, f32[4096,128]{0,1:T(8,128)} %fusion.37, f32[4096,128]{0,1:T(8,128)} %convolution_multiply_fusion.2), kind=kLoop, calls=%fused_computation.64 | loop fusion | flops 2097152 | bytes 12582912 | tf_op jit(solution)/shard_map/add | solution.py:142
  167.6 2.8 copy.17
  170.4 1.0 fusion.36
  171.5 120.1 %reduce-scatter.2.cloned.1.call-done = f32[128,256]{0,1:T(8,128)} async-done(((f32[4096,256]{0,1:T(8,128)}), f32[128,256]{0,1:T(8,128)}) %reduce-scatter.2.cloned.1.call-update) | async-done | bytes 131088 | tf_op jit(solution)/shard_map/reduce_scatter | solution.py:146
  291.6 76.6 %all-reduce.2 = (bf16[128,256]{0,1:T(8,128)(2,1)S(1)}, bf16[1024,256]{1,0:T(8,128)(2,1)}) all-reduce(f32[128,256]{0,1:T(8,128)} %reduce-scatter.2.cloned.1.call-done, f32[1024,256]{1,0:T(8,128)} %copy.17), channel_id=1, replica_groups=mesh['seq'=32,'head'=8] {'head'}, use_global_device_ids=true, to_apply=%region_12.13 | all-reduce | flops 294912 | bytes 1769472 | tf_op jit(solution)/shard_map/psum | solution.py:147
  (78 shorter events, 12.7 us)
Async XLA Ops:
  7.2 85.6 %copy-start = (bf16[128,128]{1,0:T(8,128)(2,1)S(1)}, bf16[128,128]{1,0:T(8,128)(2,1)}, u32[]{:S(2)}) copy-start(bf16[128,128]{1,0:T(8,128)(2,1)} %param.9) | copy-start | bytes 98308
  7.2 85.6 %all-gather.2.cloned.1.call-start = ((), (), s32[]{:S(2)}) async-start(), calls=%async_computation.1 | async-start | bytes 2162688 | tf_op jit(solution)/shard_map/all_gather | solution.py:119
  7.9 283.7 %reduce-scatter.2.cloned.1.call-start = ((), (), s32[]{:S(2)}) async-start(), calls=%async_computation.2 | async-start | bytes 4325376 | tf_op jit(solution)/shard_map/reduce_scatter | solution.py:146
  95.2 0.8 copy-start.15
  96.0 1.9 copy-start.5
  98.9 2.0 copy-start.9
  100.7 0.9 copy-start.11
  100.8 1.1 copy-start.14
  100.8 1.2 copy-start.16
  101.9 8.4 %copy-start.12 = (bf16[4096,128]{1,0:T(8,128)(2,1)}, bf16[4096,128]{1,0:T(8,128)(2,1)S(1)}, u32[]{:S(2)}) copy-start(bf16[4096,128]{1,0:T(8,128)(2,1)S(1)} %get-tuple-element.70) | copy-start | bytes 3145732 | tf_op jit(solution)/shard_map/cond
  101.9 8.4 %copy-start.17 = (bf16[1024,128]{1,0:T(8,128)(2,1)}, bf16[1024,128]{1,0:T(8,128)(2,1)S(1)}, u32[]{:S(2)}) copy-start(bf16[1024,128]{1,0:T(8,128)(2,1)S(1)} %get-tuple-element.115) | copy-start | bytes 786436 | tf_op jit(solution)/shard_map/cond
  103.7 6.7 %copy-start.19 = (bf16[1024,128]{1,0:T(8,128)(2,1)}, bf16[1024,128]{1,0:T(8,128)(2,1)S(1)}, u32[]{:S(2)}) copy-start(bf16[1024,128]{1,0:T(8,128)(2,1)S(1)} %get-tuple-element.145) | copy-start | bytes 786436 | tf_op jit(solution)/shard_map/cond
  109.7 2.6 copy-start.7
  112.3 4.0 %copy-start.2 = (f32[5120,512]{1,0:T(8,128)}, f32[5120,512]{1,0:T(8,128)S(1)}, u32[]{:S(2)}) copy-start(f32[5120,512]{1,0:T(8,128)S(1)} %get-tuple-element.149) | copy-start | bytes 31457284 | tf_op jit(solution)/shard_map/cond
  120.1 4.0 %copy-start.3 = (f32[5120,512]{1,0:T(8,128)S(1)}, f32[5120,512]{1,0:T(8,128)}, u32[]{:S(2)}) copy-start(f32[5120,512]{1,0:T(8,128)} %copy-done.2) | copy-start | bytes 31457284 | tf_op jit(solution)/shard_map/cond
  120.1 4.1 %copy-start.8 = (pred[512,1024]{0,1:T(32,128)(4,1)S(1)}, pred[512,1024]{0,1:T(32,128)(4,1)}, u32[]{:S(2)}) copy-start(pred[512,1024]{0,1:T(32,128)(4,1)} %copy-done.7) | copy-start | bytes 1572868 | tf_op jit(solution)/shard_map/cond
  129.9 3.8 %copy-start.13 = (bf16[4096,128]{1,0:T(8,128)(2,1)S(1)}, bf16[4096,128]{1,0:T(8,128)(2,1)}, u32[]{:S(2)}) copy-start(bf16[4096,128]{1,0:T(8,128)(2,1)} %copy-done.12) | copy-start | bytes 3145732 | tf_op jit(solution)/shard_map/cond
  129.9 3.8 %copy-start.20 = (bf16[1024,128]{1,0:T(8,128)(2,1)S(1)}, bf16[1024,128]{1,0:T(8,128)(2,1)}, u32[]{:S(2)}) copy-start(bf16[1024,128]{1,0:T(8,128)(2,1)} %copy-done.19) | copy-start | bytes 786436 | tf_op jit(solution)/shard_map/cond
  146.5 3.8 %slice-start.2 = ((s8[5242880]{0:T(1024)(128)(4,1)}), s8[1048576]{0:T(1024)(128)(4,1)S(1)}, s32[]{:S(2)}) async-start(s8[5242880]{0:T(1024)(128)(4,1)} %bitcast.42), calls=%async_computation.5 | async-start | bytes 2097152 | tf_op jit(solution)/shard_map/cond
  148.4 2.2 slice-start.3
  148.4 2.2 copy-start.18
  150.3 2.1 copy-start.4
  150.3 3.2 slice-start
  150.6 3.1 slice-start.1
  155.5 1.6 slice-start.4
  157.1 2.5 slice-start.5
  166.9 3.5 copy-start.6
  166.9 3.5 copy-start.10
  167.6 201.3 %copy-start.1 = (bf16[128,128]{1,0:T(8,128)(2,1)S(1)}, bf16[128,128]{1,0:T(8,128)(2,1)}, u32[]{:S(2)}) copy-start(bf16[128,128]{1,0:T(8,128)(2,1)} %param.9) | copy-start | bytes 98308
Sparse Core Ops, SparseCore 0:
  10.8 81.9 all-gather.1
  167.0 124.5 reduce-scatter.1
where the time goes:
time: 377 us; the launch traced here: 376 us
  waiting for transfers between devices  204 us (54%)
  blocking collectives  76.6 us (20%)
  matrix products  37.8 us (10%)
  other arithmetic  27.7 us (7%)
  between operations  14.8 us (4%)
  local copies, waits for them, and re-layouts  14.3 us (4%)
    reduce_scatter x1, waiting for transfers between devices, on_device(): lax.psum_scatter(prompt_part, 'seq', scatter_dimension=0, tiled=True)  120 us
    all_gather x1, waiting for transfers between devices, on_device(): whole = lax.all_gather(prompt_cache, 'seq', axis=0, tiled=True)  83.3 us
    psum x1, blocking collectives, on_device(): prompt_sum = lax.psum(share_sum, 'head')  76.6 us
    dot_general x3, matrix products, head_pass(): jnp.dot(score_grad, keys, preferred_element_type=jnp.float32) * scale  9.15 us
    dot_general x3, matrix products, head_pass(): slopes = jnp.dot(cotangent, values.T, preferred_element_type=jnp.float32)  8.16 us
  transfers between devices with their start and end apart: 2, of which 2 were waited for; matrix products, arithmetic and copies ran while one was open for 1% of the time, Pallas kernels for 0%

commit v1 on v0

v1 whole, which is shorter than its diff:
```python
import functools, math
import jax, jax.numpy as jnp
from jax import lax
from jax.experimental import pallas as pl
from jax.experimental.pallas import tpu as pltpu
f32=jnp.float32; bf16=jnp.bfloat16
HDIM=128

def dot(a,b): return jnp.dot(a,b,preferred_element_type=f32)

def attend(q,g,kv_at,kvt_at,segs,s_scr,pb_scr,live,add_grad,chunk):
    rb=q.shape[0]
    c=math.log2(math.e)/math.sqrt(HDIM)
    qt=q.astype(f32).T.astype(bf16); gt=g.astype(f32).T.astype(bf16)
    def rows(i): return pl.ds(pl.multiple_of(i*chunk,chunk),chunk)
    m=jnp.full((8,rb),-1e30,f32)
    for (which,base,lo,hi,mask) in segs:
        def step(i,m):
            s=dot(kv_at(which,i)[:,:HDIM],qt)
            if mask is not None: s=jnp.where(mask(i),s,-1e30)
            s_scr[rows(base+i),:rb]=s
            return jnp.maximum(m,jnp.max(s.reshape(chunk//8,8,rb),axis=0))
        m=lax.fori_loop(lo,hi,step,m)
    m=jnp.max(m,axis=0,keepdims=True)
    l=jnp.zeros((8,rb),f32)
    for (which,base,lo,hi,mask) in segs:
        def step(i,l):
            e=jnp.exp2((s_scr[rows(base+i),:rb]-m)*c)
            s_scr[rows(base+i),:rb]=e
            return l+jnp.sum(e.reshape(chunk//8,8,rb),axis=0)
        l=lax.fori_loop(lo,hi,step,l)
    inv=jnp.where(live,1.0/jnp.sum(l,axis=0,keepdims=True),0.0)
    ot=jnp.zeros((HDIM,rb),f32)
    for (which,base,lo,hi,mask) in segs:
        def step(i,ot):
            p=s_scr[rows(base+i),:rb]*inv
            pb=p.astype(bf16)
            pb_scr[rows(base+i),:rb]=pb
            return ot+dot(kvt_at(which,i)[HDIM:],pb)
        ot=lax.fori_loop(lo,hi,step,ot)
    delta=jnp.sum(gt.astype(f32)*ot,axis=0,keepdims=True)
    dqt=jnp.zeros((HDIM,rb),f32)
    for (which,base,lo,hi,mask) in segs:
        def step(i,dqt):
            dp=dot(kv_at(which,i)[:,HDIM:],gt)
            p=s_scr[rows(base+i),:rb]*inv
            ds=(p*(dp-delta)).astype(bf16)
            dv=dot(pb_scr[rows(base+i),:rb],g)
            dk=dot(ds,q)
            add_grad(which,i,dk,dv)
            return dqt+dot(kvt_at(which,i)[:HDIM],ds)
        dqt=lax.fori_loop(lo,hi,step,dqt)
    return ot.T.astype(bf16),(dqt*(1.0/math.sqrt(HDIM))).T.astype(bf16)

def kernel(RB,KC,info,qp,gp,kvp,qr,gr,kvr,op,dqp,our,dqr,dkv,dkvr,s_scr,pb_scr,kvt):
    length=info[0]; sidx=info[1]
    share=qp.shape[0]; count=kvp.shape[0]; span=qr.shape[0]
    nch=count//KC; nown=span//KC
    def rows(i): return pl.ds(pl.multiple_of(i*KC,KC),KC)
    def kv_at(which,i): return (kvp if which==0 else kvr)[rows(i),:]
    def kvt_at(which,i):
        return kvt[:,pl.ds(pl.multiple_of((i+(0 if which==0 else nch))*KC,KC),KC)]
    def tr(i,_):
        kvt[:,rows(i)]=kvp[rows(i),:].astype(f32).T.astype(bf16)
        return 0
    lax.fori_loop(0,nch,tr,0)
    zero=jnp.zeros((KC,2*HDIM),f32)
    def add(which,i,dk,dv):
        ref=dkv if which==0 else dkvr
        ref[rows(i),:HDIM]+=dk
        ref[rows(i),HDIM:]+=dv
    def put(which,i,dk,dv):
        ref=dkv if which==0 else dkvr
        ref[rows(i),:HDIM]=dk
        ref[rows(i),HDIM:]=dv
    def clear(i,_):
        dkv[rows(i),:]=zero
        return 0
    n=((sidx+1)*share+KC-1)//KC
    kio=lax.broadcasted_iota(jnp.int32,(KC,share),0)
    rio=lax.broadcasted_iota(jnp.int32,(KC,share),1)
    pmask=lambda i: i*KC+kio<=sidx*share+rio
    o,dq=attend(qp[...],gp[...],kv_at,kvt_at,[(0,0,0,n,pmask)],s_scr,pb_scr,True,put,KC)
    op[...]=o; dqp[...]=dq
    lax.fori_loop(n,nch,clear,0)
    @pl.when(length>0)
    def _():
        def tr2(i,_):
            kvt[:,pl.ds(pl.multiple_of((nch+i)*KC,KC),KC)]=kvr[rows(i),:].astype(f32).T.astype(bf16)
            dkvr[rows(i),:]=zero
            return 0
        lax.fori_loop(0,nown,tr2,0)
        for b in range(span//RB):
            ko=lax.broadcasted_iota(jnp.int32,(KC,RB),0)
            ro=lax.broadcasted_iota(jnp.int32,(KC,RB),1)
            omask=lambda i,b=b: i*KC+ko<=b*RB+ro
            live=b*RB+lax.broadcasted_iota(jnp.int32,(1,RB),1)<length
            full=(b*RB)//KC
            end=((b+1)*RB)//KC
            segs=[(0,0,0,nch,None)]
            if full>0: segs.append((1,nch,0,full,None))
            segs.append((1,nch,full,end,omask))
            o,dq=attend(qr[b*RB:(b+1)*RB,:],gr[b*RB:(b+1)*RB,:],kv_at,kvt_at,segs,s_scr,pb_scr,live,add,KC)
            our[b*RB:(b+1)*RB,:]=o
            dqr[b*RB:(b+1)*RB,:]=dq
    @pl.when(length==0)
    def _():
        our[...]=jnp.zeros_like(our); dqr[...]=jnp.zeros_like(dqr)
        dkvr[...]=jnp.zeros_like(dkvr)

def run(info,qp,gp,kvp,qr,gr,kvr,RB=512,KC=512):
    span=qr.shape[0]; count=kvp.shape[0]
    V=pl.BlockSpec(memory_space=pltpu.VMEM)
    return pl.pallas_call(
        functools.partial(kernel,RB,KC),
        out_shape=(jax.ShapeDtypeStruct(qp.shape,bf16),jax.ShapeDtypeStruct(qp.shape,bf16),
                   jax.ShapeDtypeStruct(qr.shape,bf16),jax.ShapeDtypeStruct(qr.shape,bf16),
                   jax.ShapeDtypeStruct(kvp.shape,f32),jax.ShapeDtypeStruct(kvr.shape,f32)),
        in_specs=[pl.BlockSpec(memory_space=pltpu.SMEM)]+[V]*6,
        out_specs=(V,)*6,
        scratch_shapes=[pltpu.VMEM((count+span,RB),f32),pltpu.VMEM((count+span,RB),bf16),pltpu.VMEM((2*HDIM,count+span),bf16)],
        compiler_params=pltpu.CompilerParams(vmem_limit_bytes=60*1024*1024),
        name="attention",
    )(info,qp,gp,kvp,qr,gr,kvr)


CORES = 2


def swap_cores(x, seq):
    return lax.ppermute(x, "seq", [(i, i ^ 1) for i in range(seq)])


def spread(x, axis, groups=None):
    return lax.all_to_all(x, axis, 0, 0, tiled=True, axis_index_groups=groups)


def on_device(qp, kvp, qr, kvr, gp, gr, lengths):
    seq = lax.axis_size("seq")
    heads = lax.axis_size("head")
    me = lax.axis_index("seq")
    head = lax.axis_index("head")
    core = me % CORES
    chips = seq // CORES
    columns = [[i * CORES + c for i in range(chips)] for c in range(CORES)]
    share, wide = kvp.shape

    other = swap_cores(kvp, seq)
    both = jnp.where(core == 0, jnp.concatenate([kvp, other]), jnp.concatenate([other, kvp]))
    part = CORES * share // (CORES * heads)
    piece = lax.dynamic_slice_in_dim(both, (core * heads + head) * part, part, 0)
    piece = spread(jnp.broadcast_to(piece[None], (chips, part, wide)), "seq", columns)
    half = spread(jnp.broadcast_to(piece[None], (heads, chips, part, wide)), "head")
    other = swap_cores(half, seq)
    whole = jnp.where(core == 0, jnp.stack([half, other]), jnp.stack([other, half]))
    whole = whole.reshape(CORES * heads, chips, part, wide).transpose(1, 0, 2, 3).reshape(-1, wide)

    info = jnp.stack([lengths[0], me.astype(jnp.int32)])
    op, dqp, our, dqr, dkv, dkvr = run(info, qp, gp, whole, qr, gr, kvr)

    view = dkv.reshape(chips, CORES, share, wide)
    mine = lax.dynamic_index_in_dim(view, core, 1, False)
    give = lax.dynamic_index_in_dim(view, 1 - core, 1, False)
    chip = mine + swap_cores(give, seq)
    strip = share // heads
    chip = chip.reshape(chips, heads, strip, wide).transpose(1, 0, 2, 3).reshape(heads, -1, wide)
    own = dkvr.reshape(heads, -1, wide)
    summed = spread(jnp.concatenate([chip, own], axis=1), "head").sum(0)
    cut = chips * strip
    mixed = spread(summed[:cut].reshape(chips, strip, wide), "seq", columns).sum(0)
    scale = jnp.where(jnp.arange(wide) < wide // 2, 1.0 / math.sqrt(wide // 2), 1.0).astype(f32)
    done = (jnp.concatenate([mixed, summed[cut:]]) * scale).astype(bf16)
    done = spread(jnp.broadcast_to(done[None], (heads,) + done.shape), "head")
    return (op, our, dqp, dqr, done[:, :strip].reshape(share, wide), done[:, strip:].reshape(-1, wide))


def solution(mesh):
    P = jax.sharding.PartitionSpec
    rows, cache = P("seq", "head"), P("seq", None)
    return jax.shard_map(
        on_device,
        mesh=mesh,
        in_specs=(rows, cache, rows, cache, rows, rows, P("seq")),
        out_specs=(rows, rows, rows, rows, cache, cache),
        check_vma=False,
    )
```

time: 377 us -> 168 us (0.45)
  waiting for transfers between devices: 204 us -> 18.3 us
  matrix products: 37.8 us -> 0 us
  Pallas kernels: 0 us -> 32.5 us
  other arithmetic: 27.7 us -> 3.97 us
  blocking collectives: 76.6 us -> 92.5 us
  between operations: 14.8 us -> 1.42 us
  starting transfers between devices: 0.08 us -> 9.48 us
  local copies, waits for them, and re-layouts: 14.3 us -> 8.18 us
    reduce_scatter x1 -> x0, waiting for transfers between devices: 120 us -> none  [on_device(): lax.psum_scatter(prompt_part, 'seq', scatter_dimension=0, tiled=True)]
    all_to_all x0 -> x4, blocking collectives: none -> 92.5 us  [spread(): return lax.all_to_all(x, axis, 0, 0, tiled=True, axis_index_groups=groups)]
    all_gather x1 -> x0, waiting for transfers between devices: 83.3 us -> none  [on_device(): whole = lax.all_gather(prompt_cache, 'seq', axis=0, tiled=True)]
    psum x1 -> x0, blocking collectives: 76.6 us -> none  [on_device(): prompt_sum = lax.psum(share_sum, 'head')]
    dot_general x18 -> x0, matrix products: 37.8 us -> none  [the longest x3 9.15 us: head_pass(): jnp.dot(score_grad, keys, preferred_element_type=jnp.float32) * scale]
    pallas_call x0 -> x1, Pallas kernels: none -> 32.5 us  [run(): pl.pallas_call(functools.partial(kernel, RB, KC), out_shape=(jax.ShapeDty...]
    all_to_all x0 -> x1, waiting for transfers between devices: none -> 11.1 us  [spread(): return lax.all_to_all(x, axis, 0, 0, tiled=True, axis_index_groups=groups)]
    all_to_all x0 -> x1, starting transfers between devices: none -> 9.38 us  [spread(): return lax.all_to_all(x, axis, 0, 0, tiled=True, axis_index_groups=groups)]
  transfers between devices with their start and end apart: 2 -> 4, of which waited for: 2 -> 4; matrix products, arithmetic and copies ran while one was open for 1% -> 0% of each run, Pallas kernels for 0% -> 0%
where the time goes in v1:
time: 168 us; the launch traced here: 166 us
  blocking collectives  92.5 us (55%)
  Pallas kernels  32.5 us (19%)
  waiting for transfers between devices  18.3 us (11%)
  starting transfers between devices  9.48 us (6%)
  local copies, waits for them, and re-layouts  8.18 us (5%)
  other arithmetic  3.97 us (2%)
    all_to_all x4, blocking collectives, spread(): return lax.all_to_all(x, axis, 0, 0, tiled=True, axis_index_groups=groups)  92.5 us
    pallas_call x1, Pallas kernels, run(): pl.pallas_call(functools.partial(kernel, RB, KC), out_shape=(jax.ShapeDty...  32.5 us
    all_to_all x1, waiting for transfers between devices, spread(): return lax.all_to_all(x, axis, 0, 0, tiled=True, axis_index_groups=groups)  11.1 us
    all_to_all x1, starting transfers between devices, spread(): return lax.all_to_all(x, axis, 0, 0, tiled=True, axis_index_groups=groups)  9.38 us
    ppermute x3, waiting for transfers between devices, swap_cores(): return lax.ppermute(x, 'seq', [(i, i ^ 1) for i in range(seq)])  7.21 us
  transfers between devices with their start and end apart: 4, of which 4 were waited for; matrix products, arithmetic and copies ran while one was open for 0% of the time, Pallas kernels for 0%

profile of v1, /device:TPU:2, one launch (start us, length us, event | category | flops | bytes accessed | tf_op | source)
XLA Modules:
  0.0 166.3 jit_solution(6313525209017539434)
XLA Ops:
  0.6 0.1 collective-permute-start
  0.8 1.4 collective-permute-done
  2.2 0.7 fusion.3
  2.9 20.2 %all_to_all.25 = bf16[16,16,256]{2,1,0:T(8,128)(2,1)S(1)} all-to-all(bf16[16,16,256]{2,1,0:T(8,128)(2,1)S(1)} %broadcast_in_dim.14), channel_id=1, replica_groups={{0,16,32,48,64,80,96,112,128,144,160,176,192,208,224,240},{8,24,40,56,7..., dimensions={0} | all-to-all | bytes 262144 | tf_op jit(solution)/shard_map/all_to_all | solution.py:135
  23.1 0.1 broadcast_in_dim.15
  23.2 19.0 %all_to_all.26 = bf16[8,16,16,256]{3,2,1,0:T(8,128)(2,1)S(1)} all-to-all(bf16[8,16,16,256]{3,2,1,0:T(8,128)(2,1)S(1)} %broadcast_in_dim.15), channel_id=1, replica_groups=mesh['seq'=32,'head'=8] {'head'}, dimensions={0} | all-to-all | bytes 2097152 | tf_op jit(solution)/shard_map/all_to_all | solution.py:135
  42.2 0.0 collective-permute-start.1
  42.8 0.6 pad_add_fusion.info
  43.4 1.4 collective-permute-done.1
  44.8 0.3 maximum_select_fusion
  45.2 1.5 copy.14
  46.7 32.5 %attention.1 = (bf16[128,128]{1,0:T(8,128)(2,1)}, bf16[128,128]{1,0:T(8,128)(2,1)}, bf16[1024,128]{1,0:T(8,128)(2,1)}, bf16[1024,128]{1,0:T(8,128)(2,1)}, f32[4096,256]{1,0:T(8,128)}, /*index=5*/f32[1024,256]{1,0:T(8,128)}) custom-call(s32[2]{0:T(128)} %pad_add_fusion.info, bf16[128,128]{1,0:T(8,128)(2,1)} %qp.1, bf16[128,128]{1,0:T(8,128)(2,1)} %gp.1, ...), custom_call_target="tpu_custom_call" | custom-call | tf_op jit(solution)/shard_map/attention/pallas_call | solution.py:114
  79.3 3.1 %dynamic-slice_bitcast_fusion = f32[16,128,256]{2,1,0:T(8,128)} fusion(f32[16,2,128,256]{3,2,1,0:T(8,128)} %bitcast.24, s32[]{:T(128)S(6)} %select_n.53), kind=kLoop, calls=%fused_computation.3 | loop fusion | bytes 4194308 | tf_op jit(solution)/shard_map/jit(dynamic_index_in_dim)/squeeze | solution.py:163
  82.4 0.0 collective-permute-start.2
  82.4 4.4 %collective-permute-done.2 = f32[16,128,256]{2,1,0:T(8,128)S(1)} collective-permute-done((f32[16,128,256]{2,1,0:T(8,128)}, f32[16,128,256]{2,1,0:T(8,128)S(1)}, u32[]{:S(2)}, u32[]{:S(2)}) %collective-permute-start.2) | collective-permute-done | bytes 2097184 | tf_op jit(solution)/shard_map/ppermute | solution.py:131
  86.7 1.9 %bitcast_add_fusion = f32[16,128,256]{2,1,0:T(8,128)S(1)} fusion(f32[16,128,256]{2,1,0:T(8,128)S(1)} %collective-permute-done.2, f32[16,2,128,256]{3,2,1,0:T(8,128)} %bitcast.25, s32[]{:T(128)S(6)} %select_n.52), kind=kLoop, calls=%fused_computation.2 | loop fusion | flops 524288 | bytes 6291460 | tf_op jit(solution)/shard_map/add | solution.py:164
  88.6 0.0 copy-start
  88.6 0.2 copy.15
  88.8 1.0 copy-done
  89.8 0.2 pad_maximum_fusion
  90.0 41.3 %all_to_all.27 = f32[8,384,256]{2,1,0:T(8,128)S(1)} all-to-all(f32[8,384,256]{2,1,0:T(8,128)S(1)} %pad_maximum_fusion), channel_id=1, replica_groups=mesh['seq'=32,'head'=8] {'head'}, dimensions={0} | all-to-all | bytes 6291456 | tf_op jit(solution)/shard_map/all_to_all | solution.py:135
  131.3 0.2 reduce_sum.18
  131.6 0.7 slice.16
  132.3 9.4 %all-to-all-start.3 = ((f32[16,16,256]{2,1,0:T(8,128)}), f32[16,16,256]{2,1,0:T(8,128)S(1)}, u32[]{:S(2)}, u32[]{:S(2)}) async-start(f32[16,16,256]{2,1,0:T(8,128)} %bitcast.13), calls=%async_computation.3 | async-start | bytes 524288 | tf_op jit(solution)/shard_map/all_to_all | solution.py:135
  141.7 11.1 %all-to-all-done.3 = f32[16,16,256]{2,1,0:T(8,128)S(1)} async-done(((f32[16,16,256]{2,1,0:T(8,128)}), f32[16,16,256]{2,1,0:T(8,128)S(1)}, u32[]{:S(2)}, u32[]{:S(2)}) %all-to-all-start.3) | async-done | bytes 262176 | tf_op jit(solution)/shard_map/all_to_all | solution.py:135
  152.9 12.0 %all_to_all.28 = bf16[8,144,256]{2,1,0:T(8,128)(2,1)S(1)} all-to-all(bf16[8,144,256]{2,1,0:T(8,128)(2,1)S(1)} %broadcast_in_dim.31), channel_id=1, replica_groups=mesh['seq'=32,'head'=8] {'head'}, dimensions={0} | all-to-all | bytes 1179648 | tf_op jit(solution)/shard_map/all_to_all | solution.py:135
  164.9 0.6 slice.18
  165.5 0.8 slice.19
  (6 shorter events, 0.1 us)
Async XLA Ops:
  0.6 1.6 collective-permute-start
  42.2 2.7 %collective-permute-start.1 = (bf16[8,16,16,256]{3,2,1,0:T(8,128)(2,1)S(1)}, bf16[8,16,16,256]{3,2,1,0:T(8,128)(2,1)S(1)}, u32[]{:S(2)}, u32[]{:S(2)}) collective-permute-start(bf16[8,16,16,256]{3,2,1,0:T(8,128)(2,1)S(1)} %all_to_all.26), channel_id=1, source_target_pairs={{0,8},{8,0},{16,24},{24,16},{32,40},{40,32},{48,56},{56,48},{64,72... | collective-permute-start | bytes 3145736 | tf_op jit(solution)/shard_map/ppermute | solution.py:131
  82.4 4.4 %collective-permute-start.2 = (f32[16,128,256]{2,1,0:T(8,128)}, f32[16,128,256]{2,1,0:T(8,128)S(1)}, u32[]{:S(2)}, u32[]{:S(2)}) collective-permute-start(f32[16,128,256]{2,1,0:T(8,128)} %dynamic-slice_bitcast_fusion), channel_id=1, source_target_pairs={{0,8},{8,0},{16,24},{24,16},{32,40},{40,32},{48,56},{56,48},{64,72... | collective-permute-start | bytes 6291464 | tf_op jit(solution)/shard_map/ppermute | solution.py:131
  88.6 1.2 copy-start
  132.3 20.5 %all-to-all-start.3 = ((f32[16,16,256]{2,1,0:T(8,128)}), f32[16,16,256]{2,1,0:T(8,128)S(1)}, u32[]{:S(2)}, u32[]{:S(2)}) async-start(f32[16,16,256]{2,1,0:T(8,128)} %bitcast.13), calls=%async_computation.3 | async-start | bytes 524288 | tf_op jit(solution)/shard_map/all_to_all | solution.py:135

commit v2 on v1

v2 whole, which is shorter than its diff:
```python
import functools, math
import jax, jax.numpy as jnp
from jax import lax
from jax.experimental import pallas as pl
from jax.experimental.pallas import tpu as pltpu
f32=jnp.float32; bf16=jnp.bfloat16
D=128
RATE=math.log2(math.e)/math.sqrt(D)
FAR=1e30
OWN=256
SEQ=("x_hi","z","core")
HEAD=("y","x_lo")
PLANE=("x_hi","y","x_lo")
LONG=8
HEADS=8
CORE_CHIPS=16
ROWS=16

def dot(a,b): return jnp.dot(a,b,preferred_element_type=f32)
def flip(x): return x.astype(f32).T.astype(bf16)
def fold(x): return x.reshape(x.shape[0]//8,8,x.shape[1])
def rows(i,n): return pl.ds(i*n,n)
def loop(n,step,init):
    for i in range(n): init=step(i,init)
    return init

def key_place(core,start,n,share,strip):
    r=start+lax.broadcasted_iota(jnp.int32,(n,share),0)
    wide=lambda size: size.bit_length()-1
    x=r>>wide(strip*CORE_CHIPS//2); head=(r>>wide(strip))&(HEADS-1); z=(r>>wide(ROWS))&(LONG-1); t=r&(ROWS-1)
    return ((x*LONG+z)*2+core)*share+head*ROWS+t

def forward(KC,info,qp,gp,near,far,qr,gr,kvr,op,our,stat,dqo,dkvr,s,own):
    length=info[0]; first=info[1]*qp.shape[0]
    half=near.shape[0]; count=2*half; span=qr.shape[0]; share=qp.shape[0]; n=span+share
    qt=jnp.concatenate([flip(qr[...]),flip(qp[...])],axis=1)
    gt=jnp.concatenate([flip(gr[...]),flip(gp[...])],axis=1)
    def part(i):
        return (near if i*KC<half else far)[pl.ds(i*KC%half,KC),:]
    def seen(i):
        place=key_place(info[2] if i*KC<half else 1-info[2],i*KC%half,KC,share,half//CORE_CHIPS)
        return place<=first+lax.broadcasted_iota(jnp.int32,(KC,share),1)
    tri=lax.broadcasted_iota(jnp.int32,(OWN,OWN),0)<=lax.broadcasted_iota(jnp.int32,(OWN,OWN),1)
    def top(i,m):
        x=dot(part(i)[:,:D],qt)
        x=jnp.concatenate([x[:,:span],jnp.where(seen(i),x[:,span:],-FAR)],axis=1)
        s[rows(i,KC),:]=x
        return jnp.maximum(m,jnp.max(fold(x),axis=0))
    m=loop(count//KC,top,jnp.full((8,n),-FAR,f32))
    mr=m[:,:span]
    for j in range(span//OWN):
        x=dot(kvr[j*OWN:(j+1)*OWN,:D],qt[:,j*OWN:span])
        d=jnp.where(tri,x[:,:OWN],-FAR)
        x=d if x.shape[1]==OWN else jnp.concatenate([d,x[:,OWN:]],axis=1)
        own[j*OWN:(j+1)*OWN,j*OWN:span]=x
        y=jnp.max(fold(x),axis=0)
        y=jnp.maximum(mr[:,j*OWN:],y)
        mr=y if j==0 else jnp.concatenate([mr[:,:j*OWN],y],axis=1)
    m=jnp.max(jnp.concatenate([mr,m[:,span:]],axis=1),axis=0,keepdims=True)*RATE
    def total(i,l):
        return l+jnp.sum(fold(jnp.exp2(s[rows(i,KC),:]*RATE-m)),axis=0)
    l=loop(count//KC,total,jnp.zeros((8,n),f32))
    lr=l[:,:span]
    for j in range(span//OWN):
        y=lr[:,j*OWN:]+jnp.sum(fold(jnp.exp2(own[j*OWN:(j+1)*OWN,j*OWN:span]*RATE-m[:,j*OWN:span])),axis=0)
        lr=y if j==0 else jnp.concatenate([lr[:,:j*OWN],y],axis=1)
    l=jnp.sum(jnp.concatenate([lr,l[:,span:]],axis=1),axis=0,keepdims=True)
    level=m+jnp.log2(l)
    at=lax.broadcasted_iota(jnp.int32,(1,n),1)
    level=jnp.where((at<length)|(at>=span),level,FAR)
    def attend(i,o):
        p=jnp.exp2(s[rows(i,KC),:]*RATE-level).astype(bf16)
        return o+dot(flip(part(i)[:,D:]),p)
    o=loop(count//KC,attend,jnp.zeros((D,n),f32))
    tail=o[:,span:]
    o=o[:,:span]
    for j in range(span//OWN):
        p=jnp.exp2(own[j*OWN:(j+1)*OWN,j*OWN:span]*RATE-level[:,j*OWN:span]).astype(bf16)
        y=o[:,j*OWN:]+dot(flip(kvr[j*OWN:(j+1)*OWN,D:]),p)
        o=y if j==0 else jnp.concatenate([o[:,:j*OWN],y],axis=1)
    our[...]=o.T.astype(bf16)
    op[...]=tail.T.astype(bf16)
    delta=jnp.sum(gt.astype(f32)*jnp.concatenate([o,tail],axis=1),axis=0,keepdims=True)
    stat[...]=jnp.concatenate([jnp.broadcast_to(level,(8,n)),jnp.broadcast_to(delta,(8,n))],axis=0)
    dq=jnp.zeros((D,span),f32)
    for j in range(span//OWN):
        a=slice(j*OWN,(j+1)*OWN); b=slice(j*OWN,span)
        p=jnp.exp2(own[a,b]*RATE-level[:,b])
        dp=dot(kvr[a,D:],gt[:,b])
        ds=(p*(dp-delta[:,b])).astype(bf16)
        dkvr[a,D:]=dot(p.astype(bf16),gr[b,:])
        dkvr[a,:D]=dot(ds,qr[b,:])
        y=dq[:,b]+dot(flip(kvr[a,:D]),ds)
        dq=y if j==0 else jnp.concatenate([dq[:,:j*OWN],y],axis=1)
    dqo[...]=dq

def backward(KC,info,qp,gp,near,far,qr,gr,stat,dqo,dqp,dqr,dnear,dfar):
    first=info[1]*qp.shape[0]
    half=near.shape[0]; count=2*half; span=qr.shape[0]; share=qp.shape[0]; n=span+share
    qt=jnp.concatenate([flip(qr[...]),flip(qp[...])],axis=1)
    gt=jnp.concatenate([flip(gr[...]),flip(gp[...])],axis=1)
    q=jnp.concatenate([qr[...],qp[...]],axis=0)
    g=jnp.concatenate([gr[...],gp[...]],axis=0)
    level=stat[:1,:]; delta=stat[8:9,:]
    def part(i):
        return (near if i*KC<half else far)[pl.ds(i*KC%half,KC),:]
    def seen(i):
        place=key_place(info[2] if i*KC<half else 1-info[2],i*KC%half,KC,share,half//CORE_CHIPS)
        return place<=first+lax.broadcasted_iota(jnp.int32,(KC,share),1)
    def step(i,dq):
        x=dot(part(i)[:,:D],qt)
        dp=dot(part(i)[:,D:],gt)
        p=jnp.exp2(x*RATE-level)
        grad=dnear if i*KC<half else dfar
        a=pl.ds(i*KC%half,KC)
        p=jnp.concatenate([p[:,:span],jnp.where(seen(i),p[:,span:],0.0)],axis=1)
        ds=(p*(dp-delta)).astype(bf16)
        grad[a,D:]=dot(p.astype(bf16),g)
        grad[a,:D]=dot(ds,q)
        return dq+dot(flip(part(i)[:,:D]),ds)
    dq=loop(count//KC,step,jnp.concatenate([dqo[...],jnp.zeros((D,share),f32)],axis=1))
    dq=(dq*(1.0/math.sqrt(D))).T.astype(bf16)
    dqr[...]=dq[:span]; dqp[...]=dq[span:]

V=pl.BlockSpec(memory_space=pltpu.VMEM)
SM=pl.BlockSpec(memory_space=pltpu.SMEM)
def shape(s,t=f32): return jax.ShapeDtypeStruct(s,t)

def run_forward(info,qp,gp,near,far,qr,gr,kvr,KC=512):
    span=qr.shape[0]; half=near.shape[0]; share=qp.shape[0]; n=span+share
    return pl.pallas_call(functools.partial(forward,KC),
        out_shape=(shape(qp.shape,bf16),shape(qr.shape,bf16),shape((16,n)),shape((D,span)),shape(kvr.shape)),
        in_specs=[SM]+[V]*7,out_specs=(V,)*5,
        scratch_shapes=[pltpu.VMEM((2*half,n),f32),pltpu.VMEM((span,span),f32)],
        cost_estimate=pl.CostEstimate(flops=5*n*half*2*D,bytes_accessed=2**23,transcendentals=4*n*half),
        compiler_params=pltpu.CompilerParams(vmem_limit_bytes=56*1024*1024),name="forward")(info,qp,gp,near,far,qr,gr,kvr)

def run_backward(info,qp,gp,near,far,qr,gr,stat,dqo,KC=512):
    n=stat.shape[1]; half=near.shape[0]
    return pl.pallas_call(functools.partial(backward,KC),
        out_shape=(shape(qp.shape,bf16),shape(qr.shape,bf16),shape(near.shape),shape(far.shape)),
        in_specs=[SM]+[V]*8,out_specs=(V,)*4,
        cost_estimate=pl.CostEstimate(flops=10*n*half*2*D,bytes_accessed=2**23,transcendentals=2*n*half),
        compiler_params=pltpu.CompilerParams(vmem_limit_bytes=56*1024*1024),name="backward")(info,qp,gp,near,far,qr,gr,stat,dqo)

def swap(x): return lax.ppermute(x,"core",[(0,1),(1,0)])
def spread(x,axes): return lax.all_to_all(x,axes,0,0,tiled=True)
def copies(x,n): return jnp.broadcast_to(x[None],(n,)+x.shape)

def on_device(qp,kvp,qr,kvr,gp,gr,lengths):
    core=lax.axis_index("core")
    head=lax.axis_index(HEAD)
    info=jnp.stack([lengths[0],lax.axis_index(SEQ).astype(jnp.int32),core.astype(jnp.int32)])
    piece=lax.dynamic_slice_in_dim(kvp,head*ROWS,ROWS,0)
    line=spread(copies(piece,LONG),"z")
    near=spread(copies(line,CORE_CHIPS),PLANE).reshape(-1,2*D)
    far=swap(near)
    op,our,stat,dqo,own=run_forward(info,qp,gp,near,far,qr,gr,kvr)
    own=spread(own.reshape(HEADS,-1,2*D),HEAD).sum(0)
    dqp,dqr,dnear,dfar=run_backward(info,qp,gp,near,far,qr,gr,stat,dqo)
    chip=dnear+swap(dfar)
    line=spread(chip.reshape(CORE_CHIPS,-1,2*D),PLANE).sum(0)
    strip=spread(line.reshape(LONG,ROWS,2*D),"z").sum(0)
    scale=jnp.where(jnp.arange(2*D)<D,1.0/math.sqrt(D),1.0).astype(f32)
    done=(jnp.concatenate([strip,own])*scale).astype(bf16)
    done=spread(copies(done,HEADS),HEAD)
    return (op,our,dqp,dqr,done[:,:ROWS].reshape(-1,2*D),done[:,ROWS:].reshape(-1,2*D))

def solution(mesh):
    P=jax.sharding.PartitionSpec
    fine=jax.sharding.Mesh(mesh.devices.reshape(2,LONG,2,4,2),SEQ+HEAD)
    rows_,cache=P(SEQ,HEAD),P(SEQ,None)
    return jax.shard_map(on_device,mesh=fine,
        in_specs=(rows_,cache,rows_,cache,rows_,rows_,P(SEQ)),
        out_specs=(rows_,rows_,rows_,rows_,cache,cache),check_vma=False)
```

time: 168 us -> 157 us (0.935)
  blocking collectives: 92.5 us -> 81.8 us
  waiting for transfers between devices: 18.3 us -> 27.5 us
  local copies, waits for them, and re-layouts: 8.18 us -> 3.44 us
  Pallas kernels: 32.5 us -> 30.8 us
    all_to_all x1 -> x2, waiting for transfers between devices: 11.1 us -> 21.9 us  [spread(): return lax.all_to_all(x, axes, 0, 0, tiled=True)]
    all_to_all x4, blocking collectives: 92.5 us -> 81.8 us  [spread(): return lax.all_to_all(x, axes, 0, 0, tiled=True)]
    squeeze x1 -> x0, local copies, waits for them, and re-layouts: 3.1 us -> none  [on_device(): give = lax.dynamic_index_in_dim(view, 1 - core, 1, False)]
    pallas_call x1 -> x2, Pallas kernels: 32.5 us -> 30.8 us  [the longest x1 16 us: run_backward(): pl.pallas_call(functools.partial(backward, KC), out_shape=(shape(qp.shape...]
    ppermute x3 -> x2, waiting for transfers between devices: 7.21 us -> 5.65 us  [swap(): return lax.ppermute(x, 'core', [(0, 1), (1, 0)])]
    all_to_all x1 -> x2, starting transfers between devices: 9.38 us -> 8.29 us  [spread(): return lax.all_to_all(x, axes, 0, 0, tiled=True)]
  transfers between devices with their start and end apart: 4 -> 4, of which waited for: 4 -> 4; matrix products, arithmetic and copies ran while one was open for 0% -> 1% of each run, Pallas kernels for 0% -> 0%
where the time goes in v2:
time: 157 us
  blocking collectives  81.8 us (52%)
  Pallas kernels  30.8 us (20%)
  waiting for transfers between devices  27.5 us (18%)
  starting transfers between devices  8.43 us (5%)
  local copies, waits for them, and re-layouts  3.44 us (2%)
  other arithmetic  3.33 us (2%)
    all_to_all x4, blocking collectives, spread(): return lax.all_to_all(x, axes, 0, 0, tiled=True)  81.8 us
    all_to_all x2, waiting for transfers between devices, spread(): return lax.all_to_all(x, axes, 0, 0, tiled=True)  21.9 us
    pallas_call x1, Pallas kernels, run_backward(): pl.pallas_call(functools.partial(backward, KC), out_shape=(shape(qp.shape...  16 us
    pallas_call x1, Pallas kernels, run_forward(): pl.pallas_call(functools.partial(forward, KC), out_shape=(shape(qp.shape,...  14.8 us
    all_to_all x2, starting transfers between devices, spread(): return lax.all_to_all(x, axes, 0, 0, tiled=True)  8.29 us
    ppermute x2, waiting for transfers between devices, swap(): return lax.ppermute(x, 'core', [(0, 1), (1, 0)])  5.65 us
  transfers between devices with their start and end apart: 4, of which 4 were waited for; matrix products, arithmetic and copies ran while one was open for 1% of the time, Pallas kernels for 0%

profile of v2, /device:TPU:2, one launch (start us, length us, event | category | flops | bytes accessed | tf_op | source)
XLA Modules:
  0.0 156.7 jit_solution(3841504181653917396)
XLA Ops:
  0.6 0.0 copy-start
  0.7 0.8 copy-done
  1.5 16.6 %all_to_all.30 = bf16[8,16,256]{2,1,0:T(8,128)(2,1)S(1)} all-to-all(bf16[8,16,256]{2,1,0:T(8,128)(2,1)S(1)} %broadcast_in_dim.14), channel_id=1, replica_groups=mesh['x_hi'=2,'z'=8,'core'=2,'y'=4,'x_lo'=2] {'z'}, dimensions={0} | all-to-all | bytes 131072 | tf_op jit(solution)/shard_map/all_to_all | solution.py:147
  18.1 0.1 broadcast_in_dim.15
  18.2 22.2 %all_to_all.31 = bf16[16,8,16,256]{3,2,1,0:T(8,128)(2,1)S(1)} all-to-all(bf16[16,8,16,256]{3,2,1,0:T(8,128)(2,1)S(1)} %broadcast_in_dim.15), channel_id=1, replica_groups=mesh['x_hi'=2,'z'=8,'core'=2,'y'=4,'x_lo'=2] {'x_hi','y','x_lo'}, dimensions={0} | all-to-all | bytes 2097152 | tf_op jit(solution)/shard_map/all_to_all | solution.py:147
  40.4 0.0 copy-start.1
  40.4 0.0 collective-permute-start
  41.1 0.6 pad_add_fusion.info
  41.6 1.4 collective-permute-done.far
  43.1 0.0 copy-done.1
  43.1 0.0 copy-start.2
  43.1 1.0 copy-done.2
  44.1 14.8 %forward.1 = (bf16[128,128]{1,0:T(8,128)(2,1)}, bf16[1024,128]{1,0:T(8,128)(2,1)}, f32[16,1152]{1,0:T(8,128)}, f32[128,1024]{1,0:T(8,128)}, f32[1024,256]{1,0:T(8,128)}) custom-call(s32[3]{0:T(128)} %pad_add_fusion.info, bf16[128,128]{1,0:T(8,128)(2,1)} %qp.3, bf16[128,128]{1,0:T(8,128)(2,1)} %gp.3, bf16[2048,256]{1,0:T(8,128)(2,1)} %bitcast.10, ...), custom_call_target="tpu_custom_call" | custom-call | flops 3019898880 | bytes 8388608 | tf_op jit(solution)/shard_map/forward/pallas_call | solution.py:131
  58.8 16.0 %backward.1 = (bf16[128,128]{1,0:T(8,128)(2,1)}, bf16[1024,128]{1,0:T(8,128)(2,1)}, f32[2048,256]{1,0:T(8,128)}, f32[2048,256]{1,0:T(8,128)}) custom-call(s32[3]{0:T(128)} %pad_add_fusion.info, bf16[128,128]{1,0:T(8,128)(2,1)} %qp.3, bf16[128,128]{1,0:T(8,128)(2,1)} %gp.3, bf16[2048,256]{1,0:T(8,128)(2,1)} %bitcast.11, bf16[2048,256]{1,0:T(8,128)(2,1)} %copy-done.2, ...), custom_call_target="tpu_custom_call" | custom-call | flops 6039797760 | bytes 8388608 | tf_op jit(solution)/shard_map/backward/pallas_call | solution.py:140
  74.9 0.1 collective-permute-start.1
  75.0 4.2 %collective-permute-done.1 = f32[2048,256]{1,0:T(8,128)S(1)} collective-permute-done((f32[2048,256]{1,0:T(8,128)}, f32[2048,256]{1,0:T(8,128)S(1)}, u32[]{:S(2)}, u32[]{:S(2)}) %collective-permute-start.1) | collective-permute-done | bytes 2097184 | tf_op jit(solution)/shard_map/ppermute | solution.py:146
  79.2 1.9 %add.19 = f32[2048,256]{1,0:T(8,128)S(1)} add(f32[2048,256]{1,0:T(8,128)} %get-tuple-element.21, f32[2048,256]{1,0:T(8,128)S(1)} %collective-permute-done.1) | non-fusion elementwise | flops 524288 | bytes 6291456 | tf_op jit(solution)/shard_map/add | solution.py:161
  81.1 31.4 %all_to_all.32 = f32[16,128,256]{2,1,0:T(8,128)S(1)} all-to-all(f32[16,128,256]{2,1,0:T(8,128)S(1)} %bitcast.8), channel_id=1, replica_groups=mesh['x_hi'=2,'z'=8,'core'=2,'y'=4,'x_lo'=2] {'x_hi','y','x_lo'}, dimensions={0} | all-to-all | bytes 4194304 | tf_op jit(solution)/shard_map/all_to_all | solution.py:147
  112.5 4.9 %all-to-all-start.4 = ((f32[8,128,256]{2,1,0:T(8,128)}), f32[8,128,256]{2,1,0:T(8,128)S(1)}, u32[]{:S(2)}, u32[]{:S(2)}) async-start(f32[8,128,256]{2,1,0:T(8,128)} %bitcast.12), calls=%async_computation.4 | async-start | bytes 2097152 | tf_op jit(solution)/shard_map/all_to_all | solution.py:147
  117.4 0.8 reduce_sum.27
  118.2 13.0 %all-to-all-done.4 = f32[8,128,256]{2,1,0:T(8,128)S(1)} async-done(((f32[8,128,256]{2,1,0:T(8,128)}), f32[8,128,256]{2,1,0:T(8,128)S(1)}, u32[]{:S(2)}, u32[]{:S(2)}) %all-to-all-start.4) | async-done | bytes 1048608 | tf_op jit(solution)/shard_map/all_to_all | solution.py:147
  131.2 3.4 %all-to-all-start.3 = ((f32[8,16,256]{2,1,0:T(8,128)}), f32[8,16,256]{2,1,0:T(8,128)S(1)}, u32[]{:S(2)}, u32[]{:S(2)}) async-start(f32[8,16,256]{2,1,0:T(8,128)} %bitcast.4), calls=%async_computation.3 | async-start | bytes 262144 | tf_op jit(solution)/shard_map/all_to_all | solution.py:147
  134.6 0.1 reduce_sum.29
  134.6 8.9 %all-to-all-done.3 = f32[8,16,256]{2,1,0:T(8,128)S(1)} async-done(((f32[8,16,256]{2,1,0:T(8,128)}), f32[8,16,256]{2,1,0:T(8,128)S(1)}, u32[]{:S(2)}, u32[]{:S(2)}) %all-to-all-start.3) | async-done | bytes 131104 | tf_op jit(solution)/shard_map/all_to_all | solution.py:147
  143.6 11.6 %all_to_all.33 = bf16[8,144,256]{2,1,0:T(8,128)(2,1)S(1)} all-to-all(bf16[8,144,256]{2,1,0:T(8,128)(2,1)S(1)} %broadcast_in_dim.31), channel_id=1, replica_groups=mesh['x_hi'=2,'z'=8,'core'=2,'y'=4,'x_lo'=2] {'y','x_lo'}, dimensions={0} | all-to-all | bytes 1179648 | tf_op jit(solution)/shard_map/all_to_all | solution.py:147
  155.2 0.6 slice.8
  155.9 0.8 slice.9
  (6 shorter events, 0.1 us)
Async XLA Ops:
  0.6 0.8 copy-start
  40.4 2.7 %copy-start.1 = (bf16[16,8,16,256]{3,2,1,0:T(8,128)(2,1)}, bf16[16,8,16,256]{3,2,1,0:T(8,128)(2,1)S(1)}, u32[]{:S(2)}) copy-start(bf16[16,8,16,256]{3,2,1,0:T(8,128)(2,1)S(1)} %all_to_all.31) | copy-start | bytes 3145732
  40.4 2.7 %collective-permute-start = (bf16[2048,256]{1,0:T(8,128)(2,1)S(1)}, bf16[2048,256]{1,0:T(8,128)(2,1)S(1)}, u32[]{:S(2)}, u32[]{:S(2)}) collective-permute-start(bf16[2048,256]{1,0:T(8,128)(2,1)S(1)} %bitcast.9), channel_id=1, source_target_pairs={{0,8},{8,0},{1,9},{9,1},{2,10},{10,2},{3,11},{11,3},{4,12},{12,4},... | collective-permute-start | bytes 3145736 | tf_op jit(solution)/shard_map/ppermute | solution.py:146
  43.1 1.0 copy-start.2
  74.9 4.4 %collective-permute-start.1 = (f32[2048,256]{1,0:T(8,128)}, f32[2048,256]{1,0:T(8,128)S(1)}, u32[]{:S(2)}, u32[]{:S(2)}) collective-permute-start(f32[2048,256]{1,0:T(8,128)} %get-tuple-element.22), channel_id=1, source_target_pairs={{0,8},{8,0},{1,9},{9,1},{2,10},{10,2},{3,11},{11,3},{4,12},{12,4},... | collective-permute-start | bytes 6291464 | tf_op jit(solution)/shard_map/ppermute | solution.py:146
  112.5 18.7 %all-to-all-start.4 = ((f32[8,128,256]{2,1,0:T(8,128)}), f32[8,128,256]{2,1,0:T(8,128)S(1)}, u32[]{:S(2)}, u32[]{:S(2)}) async-start(f32[8,128,256]{2,1,0:T(8,128)} %bitcast.12), calls=%async_computation.4 | async-start | bytes 2097152 | tf_op jit(solution)/shard_map/all_to_all | solution.py:147
  131.2 12.4 %all-to-all-start.3 = ((f32[8,16,256]{2,1,0:T(8,128)}), f32[8,16,256]{2,1,0:T(8,128)S(1)}, u32[]{:S(2)}, u32[]{:S(2)}) async-start(f32[8,16,256]{2,1,0:T(8,128)} %bitcast.4), calls=%async_computation.3 | async-start | bytes 262144 | tf_op jit(solution)/shard_map/all_to_all | solution.py:147

commit v3 on v2

--- a/solution.py
+++ b/solution.py
@@ -13,6 +13,7 @@
 PLANE=("x_hi","y","x_lo")
 LONG=8
 HEADS=8
+TILE=16
 CORE_CHIPS=16
 ROWS=16
 
@@ -30,15 +31,19 @@
     x=r>>wide(strip*CORE_CHIPS//2); head=(r>>wide(strip))&(HEADS-1); z=(r>>wide(ROWS))&(LONG-1); t=r&(ROWS-1)
     return ((x*LONG+z)*2+core)*share+head*ROWS+t
 
-def forward(KC,info,qp,gp,near,far,qr,gr,kvr,op,our,stat,dqo,dkvr,s,own):
-    length=info[0]; first=info[1]*qp.shape[0]
+def seq_place():
+    return (lax.axis_index(SEQ[0])*LONG+lax.axis_index(SEQ[1]))*2+lax.axis_index(SEQ[2])
+
+def forward(KC,info,qp,gp,near,far,qr,gr,kvr,op,our,stat,dqo,own2,s,own):
+    length=info[0]; first=seq_place()*qp.shape[0]
+    core=lax.axis_index("core")
     half=near.shape[0]; count=2*half; span=qr.shape[0]; share=qp.shape[0]; n=span+share
     qt=jnp.concatenate([flip(qr[...]),flip(qp[...])],axis=1)
     gt=jnp.concatenate([flip(gr[...]),flip(gp[...])],axis=1)
     def part(i):
         return (near if i*KC<half else far)[pl.ds(i*KC%half,KC),:]
     def seen(i):
-        place=key_place(info[2] if i*KC<half else 1-info[2],i*KC%half,KC,share,half//CORE_CHIPS)
+        place=key_place(core if i*KC<half else 1-core,i*KC%half,KC,share,half//CORE_CHIPS)
         return place<=first+lax.broadcasted_iota(jnp.int32,(KC,share),1)
     tri=lax.broadcasted_iota(jnp.int32,(OWN,OWN),0)<=lax.broadcasted_iota(jnp.int32,(OWN,OWN),1)
     def top(i,m):
@@ -88,83 +93,100 @@
         p=jnp.exp2(own[a,b]*RATE-level[:,b])
         dp=dot(kvr[a,D:],gt[:,b])
         ds=(p*(dp-delta[:,b])).astype(bf16)
-        dkvr[a,D:]=dot(p.astype(bf16),gr[b,:])
-        dkvr[a,:D]=dot(ds,qr[b,:])
+        dv=dot(p.astype(bf16),gr[b,:])
+        dk=dot(ds,qr[b,:])
+        strip=span//HEADS
+        for t in range(OWN//strip):
+            u=slice(t*strip,(t+1)*strip)
+            own2[j*(OWN//strip)+t,:,D:]=dv[u]
+            own2[j*(OWN//strip)+t,:,:D]=dk[u]
         y=dq[:,b]+dot(flip(kvr[a,:D]),ds)
         dq=y if j==0 else jnp.concatenate([dq[:,:j*OWN],y],axis=1)
-    dqo[...]=dq
+    dqo[...]=jnp.concatenate([dq,jnp.zeros((D,share),f32)],axis=1)
 
-def backward(KC,info,qp,gp,near,far,qr,gr,stat,dqo,dqp,dqr,dnear,dfar):
-    first=info[1]*qp.shape[0]
-    half=near.shape[0]; count=2*half; span=qr.shape[0]; share=qp.shape[0]; n=span+share
+def backward(KC,last,qp,gp,kv,qr,gr,stat,dqo,dq_out,grad):
+    first=seq_place()*qp.shape[0]
+    core=lax.axis_index("core")
+    if not last: core=1-core
+    half=kv.shape[0]; span=qr.shape[0]; share=qp.shape[0]
     qt=jnp.concatenate([flip(qr[...]),flip(qp[...])],axis=1)
     gt=jnp.concatenate([flip(gr[...]),flip(gp[...])],axis=1)
     q=jnp.concatenate([qr[...],qp[...]],axis=0)
     g=jnp.concatenate([gr[...],gp[...]],axis=0)
     level=stat[:1,:]; delta=stat[8:9,:]
-    def part(i):
-        return (near if i*KC<half else far)[pl.ds(i*KC%half,KC),:]
     def seen(i):
-        place=key_place(info[2] if i*KC<half else 1-info[2],i*KC%half,KC,share,half//CORE_CHIPS)
+        place=key_place(core,i*KC,KC,share,half//CORE_CHIPS)
         return place<=first+lax.broadcasted_iota(jnp.int32,(KC,share),1)
     def step(i,dq):
-        x=dot(part(i)[:,:D],qt)
-        dp=dot(part(i)[:,D:],gt)
+        a=rows(i,KC)
+        x=dot(kv[a,:D],qt)
+        dp=dot(kv[a,D:],gt)
         p=jnp.exp2(x*RATE-level)
-        grad=dnear if i*KC<half else dfar
-        a=pl.ds(i*KC%half,KC)
         p=jnp.concatenate([p[:,:span],jnp.where(seen(i),p[:,span:],0.0)],axis=1)
         ds=(p*(dp-delta)).astype(bf16)
         grad[a,D:]=dot(p.astype(bf16),g)
         grad[a,:D]=dot(ds,q)
-        return dq+dot(flip(part(i)[:,:D]),ds)
-    dq=loop(count//KC,step,jnp.concatenate([dqo[...],jnp.zeros((D,share),f32)],axis=1))
-    dq=(dq*(1.0/math.sqrt(D))).T.astype(bf16)
-    dqr[...]=dq[:span]; dqp[...]=dq[span:]
+        return dq+dot(flip(kv[a,:D]),ds)
+    dq=loop(half//KC,step,dqo[...])
+    if not last: dq_out[...]=dq
+    else: dq_out[...]=(dq*(1.0/math.sqrt(D))).T.astype(bf16)
 
 V=pl.BlockSpec(memory_space=pltpu.VMEM)
 SM=pl.BlockSpec(memory_space=pltpu.SMEM)
 def shape(s,t=f32): return jax.ShapeDtypeStruct(s,t)
 
-def run_forward(info,qp,gp,near,far,qr,gr,kvr,KC=512):
+def run_forward(lengths,qp,gp,near,far,qr,gr,kvr,KC=512):
     span=qr.shape[0]; half=near.shape[0]; share=qp.shape[0]; n=span+share
     return pl.pallas_call(functools.partial(forward,KC),
-        out_shape=(shape(qp.shape,bf16),shape(qr.shape,bf16),shape((16,n)),shape((D,span)),shape(kvr.shape)),
+        out_shape=(shape(qp.shape,bf16),shape(qr.shape,bf16),shape((16,n)),shape((D,n)),shape((HEADS,span//HEADS,2*D))),
         in_specs=[SM]+[V]*7,out_specs=(V,)*5,
         scratch_shapes=[pltpu.VMEM((2*half,n),f32),pltpu.VMEM((span,span),f32)],
         cost_estimate=pl.CostEstimate(flops=5*n*half*2*D,bytes_accessed=2**23,transcendentals=4*n*half),
-        compiler_params=pltpu.CompilerParams(vmem_limit_bytes=56*1024*1024),name="forward")(info,qp,gp,near,far,qr,gr,kvr)
+        compiler_params=pltpu.CompilerParams(vmem_limit_bytes=46*1024*1024),name="forward")(lengths,qp,gp,near,far,qr,gr,kvr)
 
-def run_backward(info,qp,gp,near,far,qr,gr,stat,dqo,KC=512):
-    n=stat.shape[1]; half=near.shape[0]
-    return pl.pallas_call(functools.partial(backward,KC),
-        out_shape=(shape(qp.shape,bf16),shape(qr.shape,bf16),shape(near.shape),shape(far.shape)),
-        in_specs=[SM]+[V]*8,out_specs=(V,)*4,
-        cost_estimate=pl.CostEstimate(flops=10*n*half*2*D,bytes_accessed=2**23,transcendentals=2*n*half),
-        compiler_params=pltpu.CompilerParams(vmem_limit_bytes=56*1024*1024),name="backward")(info,qp,gp,near,far,qr,gr,stat,dqo)
+def run_backward(last,qp,gp,kv,qr,gr,stat,dqo,KC=512):
+    n=stat.shape[1]; half=kv.shape[0]
+    return pl.pallas_call(functools.partial(backward,KC,last),
+        out_shape=(shape((n,D),bf16) if last else shape((D,n)),shape(kv.shape)),
+        in_specs=[V]*7,out_specs=(V,)*2,
+        cost_estimate=pl.CostEstimate(flops=50*n*half*2*D,bytes_accessed=2**22,transcendentals=n*half),
+        compiler_params=pltpu.CompilerParams(vmem_limit_bytes=28*1024*1024),name="backward")(qp,gp,kv,qr,gr,stat,dqo)
 
 def swap(x): return lax.ppermute(x,"core",[(0,1),(1,0)])
 def spread(x,axes): return lax.all_to_all(x,axes,0,0,tiled=True)
 def copies(x,n): return jnp.broadcast_to(x[None],(n,)+x.shape)
 
+def pack(x):
+    top=jnp.maximum(jnp.max(jnp.abs(x),axis=1,keepdims=True),2.0**-100)
+    power=jnp.ceil(jnp.log2(top))
+    rest=jnp.broadcast_to(power,(x.shape[0],TILE,x.shape[2]))
+    return jnp.concatenate([x*jnp.exp2(-power),rest],axis=1).astype(jnp.float16)
+
+def unpack_sum(x):
+    power=x[:,-1:].astype(f32)
+    return jnp.sum(x[:,:-TILE].astype(f32)*jnp.exp2(power),axis=0)
+
 def on_device(qp,kvp,qr,kvr,gp,gr,lengths):
-    core=lax.axis_index("core")
     head=lax.axis_index(HEAD)
-    info=jnp.stack([lengths[0],lax.axis_index(SEQ).astype(jnp.int32),core.astype(jnp.int32)])
+    span=qr.shape[0]
     piece=lax.dynamic_slice_in_dim(kvp,head*ROWS,ROWS,0)
     line=spread(copies(piece,LONG),"z")
     near=spread(copies(line,CORE_CHIPS),PLANE).reshape(-1,2*D)
     far=swap(near)
-    op,our,stat,dqo,own=run_forward(info,qp,gp,near,far,qr,gr,kvr)
-    own=spread(own.reshape(HEADS,-1,2*D),HEAD).sum(0)
-    dqp,dqr,dnear,dfar=run_backward(info,qp,gp,near,far,qr,gr,stat,dqo)
-    chip=dnear+swap(dfar)
-    line=spread(chip.reshape(CORE_CHIPS,-1,2*D),PLANE).sum(0)
+    op,our,stat,dq,own=run_forward(lengths,qp,gp,near,far,qr,gr,kvr)
+    own=spread(pack(own),HEAD)
+    dq,dfar=run_backward(False,qp,gp,far,qr,gr,stat,dq)
+    chip=swap(dfar)
+    dq,dnear=run_backward(True,qp,gp,near,qr,gr,stat,dq)
+    chip,own=lax.optimization_barrier((chip,own))
+    own=unpack_sum(own)
+    chip=chip+dnear
+    line=unpack_sum(spread(pack(chip.reshape(CORE_CHIPS,-1,2*D)),PLANE))
     strip=spread(line.reshape(LONG,ROWS,2*D),"z").sum(0)
     scale=jnp.where(jnp.arange(2*D)<D,1.0/math.sqrt(D),1.0).astype(f32)
     done=(jnp.concatenate([strip,own])*scale).astype(bf16)
     done=spread(copies(done,HEADS),HEAD)
-    return (op,our,dqp,dqr,done[:,:ROWS].reshape(-1,2*D),done[:,ROWS:].reshape(-1,2*D))
+    return (op,our,dq[span:],dq[:span],done[:,:ROWS].reshape(-1,2*D),done[:,ROWS:].reshape(-1,2*D))
 
 def solution(mesh):
     P=jax.sharding.PartitionSpec

time: 157 us -> 136 us (0.87)
  blocking collectives: 81.8 us -> 38.8 us
  starting transfers between devices: 8.43 us -> 19.1 us
  waiting for transfers between devices: 27.5 us -> 35.1 us
  Pallas kernels: 30.8 us -> 26 us
  other arithmetic: 3.33 us -> 7.78 us
  local copies, waits for them, and re-layouts: 3.44 us -> 6.96 us
    all_to_all x4 -> x2, blocking collectives: 81.8 us -> 38.8 us  [spread(): return lax.all_to_all(x, axes, 0, 0, tiled=True)]
    all_to_all x2 -> x4, waiting for transfers between devices: 21.9 us -> 33.1 us  [spread(): return lax.all_to_all(x, axes, 0, 0, tiled=True)]
    all_to_all x2 -> x4, starting transfers between devices: 8.29 us -> 19 us  [spread(): return lax.all_to_all(x, axes, 0, 0, tiled=True)]
    ppermute x2, waiting for transfers between devices: 5.65 us -> 2.01 us  [swap(): return lax.ppermute(x, 'core', [(0, 1), (1, 0)])]
    pallas_call x1, Pallas kernels: 14.8 us -> 12.3 us  [run_forward(): pl.pallas_call(functools.partial(forward, KC), out_shape=(shape(qp.shape,...]
    pallas_call x1 -> x2, Pallas kernels: 16 us -> 13.7 us  [run_backward(): pl.pallas_call(functools.partial(backward, KC, last), out_shape=(shape((n...]
    concatenate x0 -> x2, other arithmetic: none -> 2.27 us  [pack(): jnp.concatenate([x * jnp.exp2(-power), rest], axis=1).astype(jnp.float16)]
    reduce_max x0 -> x2, other arithmetic: none -> 1.98 us  [pack(): top = jnp.maximum(jnp.max(jnp.abs(x), axis=1, keepdims=True), 2.0 ** (-100))]
  transfers between devices with their start and end apart: 4 -> 6, of which waited for: 4 -> 4; matrix products, arithmetic and copies ran while one was open for 1% -> 2% of each run, Pallas kernels for 0% -> 10%
where the time goes in v3:
time: 136 us; the launch traced here: 135 us
  blocking collectives  38.8 us (29%)
  waiting for transfers between devices  35.1 us (26%)
  Pallas kernels  26 us (19%)
  starting transfers between devices  19.1 us (14%)
  other arithmetic  7.78 us (6%)
  local copies, waits for them, and re-layouts  6.96 us (5%)
  between operations  1.5 us (1%)
    all_to_all x2, blocking collectives, spread(): return lax.all_to_all(x, axes, 0, 0, tiled=True)  38.8 us
    all_to_all x4, waiting for transfers between devices, spread(): return lax.all_to_all(x, axes, 0, 0, tiled=True)  33.1 us
    all_to_all x4, starting transfers between devices, spread(): return lax.all_to_all(x, axes, 0, 0, tiled=True)  19 us
    pallas_call x2, Pallas kernels, run_backward(): pl.pallas_call(functools.partial(backward, KC, last), out_shape=(shape((n...  13.7 us
    pallas_call x1, Pallas kernels, run_forward(): pl.pallas_call(functools.partial(forward, KC), out_shape=(shape(qp.shape,...  12.3 us
    unnamed x28, local copies, waits for them, and re-layouts  3.16 us
  transfers between devices with their start and end apart: 6, of which 4 were waited for; matrix products, arithmetic and copies ran while one was open for 2% of the time, Pallas kernels for 10%

profile of v3, /device:TPU:2, one launch (start us, length us, event | category | flops | bytes accessed | tf_op | source)
XLA Modules:
  0.0 135.2 jit_solution(2030047304151167874)
XLA Ops:
  0.7 0.8 copy-done
  1.5 16.6 %all_to_all.30 = bf16[8,16,256]{2,1,0:T(8,128)(2,1)S(1)} all-to-all(bf16[8,16,256]{2,1,0:T(8,128)(2,1)S(1)} %broadcast_in_dim.16), channel_id=1, replica_groups=mesh['x_hi'=2,'z'=8,'core'=2,'y'=4,'x_lo'=2] {'z'}, dimensions={0} | all-to-all | bytes 131072 | tf_op jit(solution)/shard_map/all_to_all | solution.py:156
  18.1 0.1 broadcast_in_dim.17
  18.2 22.2 %all_to_all.31 = bf16[16,8,16,256]{3,2,1,0:T(8,128)(2,1)S(1)} all-to-all(bf16[16,8,16,256]{3,2,1,0:T(8,128)(2,1)S(1)} %broadcast_in_dim.17), channel_id=1, replica_groups=mesh['x_hi'=2,'z'=8,'core'=2,'y'=4,'x_lo'=2] {'x_hi','y','x_lo'}, dimensions={0} | all-to-all | bytes 2097152 | tf_op jit(solution)/shard_map/all_to_all | solution.py:156
  41.1 2.0 %collective-permute-done.far.kv = bf16[2048,256]{1,0:T(8,128)(2,1)S(1)} collective-permute-done((bf16[2048,256]{1,0:T(8,128)(2,1)S(1)}, bf16[2048,256]{1,0:T(8,128)(2,1)S(1)}, u32[]{:S(2)}, u32[]{:S(2)}) %collective-permute-start) | collective-permute-done | bytes 1048608 | tf_op jit(solution)/shard_map/ppermute | solution.py:155
  43.1 12.3 %forward.1 = (bf16[128,128]{1,0:T(8,128)(2,1)}, bf16[1024,128]{1,0:T(8,128)(2,1)}, f32[16,1152]{1,0:T(8,128)S(1)}, f32[128,1152]{1,0:T(8,128)S(1)}, f32[8,128,256]{2,1,0:T(8,128)S(1)}) custom-call(s32[1]{0:T(128)S(6)} %copy.19.info, bf16[128,128]{1,0:T(8,128)(2,1)S(1)} %copy-done.6, bf16[128,128]{1,0:T(8,128)(2,1)S(1)} %copy-done.7, ...), custom_call_target="tpu_custom_call" | custom-call | flops 3019898880 | bytes 8388608 | tf_op jit(solution)/shard_map/forward/pallas_call | solution.py:140
  55.5 0.2 multiply_exponential_fusion.2
  55.7 0.1 multiply_convert_fusion.1
  55.9 0.4 copy-done.9
  56.3 1.0 pad_maximum_fusion.1
  57.2 5.2 %all-to-all-start.2 = ((f16[8,144,256]{2,1,0:T(8,128)(2,1)}), f16[8,144,256]{2,1,0:T(8,128)(2,1)}, u32[]{:S(2)}, u32[]{:S(2)}) async-start(f16[8,144,256]{2,1,0:T(8,128)(2,1)} %pad_maximum_fusion.1), calls=%async_computation.2 | async-start | bytes 1179648 | tf_op jit(solution)/shard_map/all_to_all | solution.py:156
  62.5 1.1 copy-done.10
  63.5 7.4 %backward.2 = (f32[128,1152]{1,0:T(8,128)S(1)}, f32[2048,256]{1,0:T(8,128)}) custom-call(bf16[128,128]{1,0:T(8,128)(2,1)S(1)} %copy-done.6, bf16[128,128]{1,0:T(8,128)(2,1)S(1)} %copy-done.7, bf16[2048,256]{1,0:T(8,128)(2,1)S(1)} %collective-permute-done.far.kv, bf16[1024,128]{1,0:T(8,128)(2,1)S(1)} %copy-done.2, bf16[1024,128]{1,0:T(8,128)(2,1)S(1)} %copy-done.4, ...), custom_call_target="tpu_custom_call" | custom-call | flops 30198988800 | bytes 4194304 | tf_op jit(solution)/shard_map/backward/pallas_call | solution.py:149
  71.0 0.9 copy-done.12
  71.8 6.3 %backward.3 = (bf16[1152,128]{1,0:T(8,128)(2,1)S(1)}, f32[2048,256]{1,0:T(8,128)S(1)}) custom-call(bf16[128,128]{1,0:T(8,128)(2,1)S(1)} %copy-done.6, bf16[128,128]{1,0:T(8,128)(2,1)S(1)} %copy-done.8, bf16[2048,256]{1,0:T(8,128)(2,1)S(1)} %bitcast.15, bf16[1024,128]{1,0:T(8,128)(2,1)S(1)} %copy-done.3, bf16[1024,128]{1,0:T(8,128)(2,1)S(1)} %copy-done.5, ...), custom_call_target="tpu_custom_call" | custom-call | flops 30198988800 | bytes 4194304 | tf_op jit(solution)/shard_map/backward/pallas_call | solution.py:149
  78.1 1.9 %abs_reduce_fusion = (f32[16,256]{1,0:T(8,128)S(1)}, f32[2048,256]{1,0:T(8,128)S(1)}) fusion(f32[2048,256]{1,0:T(8,128)} %collective-permute-done.1, f32[2048,256]{1,0:T(8,128)S(1)} %get-tuple-element.26), kind=kLoop, calls=%fused_computation.2 | loop fusion | flops 1568768 | bytes 6307840 | tf_op jit(solution)/shard_map/reduce_max | solution.py:160
  80.1 0.3 multiply_convert_fusion
  80.4 1.3 pad_maximum_fusion
  81.7 5.7 %all-to-all-start.3 = ((f16[16,144,256]{2,1,0:T(8,128)(2,1)}), f16[16,144,256]{2,1,0:T(8,128)(2,1)S(1)}, u32[]{:S(2)}, u32[]{:S(2)}) async-start(f16[16,144,256]{2,1,0:T(8,128)(2,1)} %pad_maximum_fusion), calls=%async_computation.3 | async-start | bytes 2359296 | tf_op jit(solution)/shard_map/all_to_all | solution.py:156
  87.5 19.2 %all-to-all-done.3 = f16[16,144,256]{2,1,0:T(8,128)(2,1)S(1)} async-done(((f16[16,144,256]{2,1,0:T(8,128)(2,1)}), f16[16,144,256]{2,1,0:T(8,128)(2,1)S(1)}, u32[]{:S(2)}, u32[]{:S(2)}) %all-to-all-start.3) | async-done | bytes 1179680 | tf_op jit(solution)/shard_map/all_to_all | solution.py:156
  106.8 0.9 multiply_reduce_fusion
  107.6 3.4 %all-to-all-start.4 = ((f32[8,16,256]{2,1,0:T(8,128)}), f32[8,16,256]{2,1,0:T(8,128)S(1)}, u32[]{:S(2)}, u32[]{:S(2)}) async-start(f32[8,16,256]{2,1,0:T(8,128)} %bitcast.2), calls=%async_computation.4 | async-start | bytes 262144 | tf_op jit(solution)/shard_map/all_to_all | solution.py:156
  111.0 0.8 multiply_exponential_fusion.1
  111.8 1.2 multiply_reduce_fusion.1
  113.0 7.0 %all-to-all-done.4 = f32[8,16,256]{2,1,0:T(8,128)S(1)} async-done(((f32[8,16,256]{2,1,0:T(8,128)}), f32[8,16,256]{2,1,0:T(8,128)S(1)}, u32[]{:S(2)}, u32[]{:S(2)}) %all-to-all-start.4) | async-done | bytes 131104 | tf_op jit(solution)/shard_map/all_to_all | solution.py:156
  120.0 0.9 broadcast_in_dim.24
  120.9 4.7 %all-to-all-start.5 = ((bf16[8,144,256]{2,1,0:T(8,128)(2,1)}), bf16[8,144,256]{2,1,0:T(8,128)(2,1)S(1)}, u32[]{:S(2)}, u32[]{:S(2)}) async-start(bf16[8,144,256]{2,1,0:T(8,128)(2,1)} %broadcast_in_dim.24), calls=%async_computation.5 | async-start | bytes 1179648 | tf_op jit(solution)/shard_map/all_to_all | solution.py:156
  125.6 0.7 slice.25
  126.3 0.6 slice.24
  126.9 6.8 %all-to-all-done.5 = bf16[8,144,256]{2,1,0:T(8,128)(2,1)S(1)} async-done(((bf16[8,144,256]{2,1,0:T(8,128)(2,1)}), bf16[8,144,256]{2,1,0:T(8,128)(2,1)S(1)}, u32[]{:S(2)}, u32[]{:S(2)}) %all-to-all-start.5) | async-done | bytes 589856 | tf_op jit(solution)/shard_map/all_to_all | solution.py:156
  133.8 0.8 slice.35
  134.6 0.6 slice.34
  (38 shorter events, 0.3 us)
Async XLA Ops:
  0.6 0.8 copy-start
  0.6 42.4 %copy-start.1 = (bf16[1024,256]{1,0:T(8,128)(2,1)S(1)}, bf16[1024,256]{1,0:T(8,128)(2,1)}, u32[]{:S(2)}) copy-start(bf16[1024,256]{1,0:T(8,128)(2,1)} %kvr.1) | copy-start | bytes 1572868
  0.7 42.4 %copy-start.7 = (bf16[128,128]{1,0:T(8,128)(2,1)S(1)}, bf16[128,128]{1,0:T(8,128)(2,1)}, u32[]{:S(2)}) copy-start(bf16[128,128]{1,0:T(8,128)(2,1)} %gp.5) | copy-start | bytes 98308
  0.7 42.4 %copy-start.4 = (bf16[1024,128]{1,0:T(8,128)(2,1)S(1)}, bf16[1024,128]{1,0:T(8,128)(2,1)}, u32[]{:S(2)}) copy-start(bf16[1024,128]{1,0:T(8,128)(2,1)} %gr.5) | copy-start | bytes 786436
  0.7 42.4 %copy-start.6 = (bf16[128,128]{1,0:T(8,128)(2,1)S(1)}, bf16[128,128]{1,0:T(8,128)(2,1)}, u32[]{:S(2)}) copy-start(bf16[128,128]{1,0:T(8,128)(2,1)} %qp.5) | copy-start | bytes 98308
  0.7 42.4 %copy-start.2 = (bf16[1024,128]{1,0:T(8,128)(2,1)S(1)}, bf16[1024,128]{1,0:T(8,128)(2,1)}, u32[]{:S(2)}) copy-start(bf16[1024,128]{1,0:T(8,128)(2,1)} %qr.5) | copy-start | bytes 786436
  40.4 2.7 %collective-permute-start = (bf16[2048,256]{1,0:T(8,128)(2,1)S(1)}, bf16[2048,256]{1,0:T(8,128)(2,1)S(1)}, u32[]{:S(2)}, u32[]{:S(2)}) collective-permute-start(bf16[2048,256]{1,0:T(8,128)(2,1)S(1)} %bitcast.13), channel_id=1, source_target_pairs={{0,8},{8,0},{1,9},{9,1},{2,10},{10,2},{3,11},{11,3},{4,12},{12,4},... | collective-permute-start | bytes 3145736 | tf_op jit(solution)/shard_map/ppermute | solution.py:155
  55.4 0.8 copy-start.9
  55.4 7.0 %copy-start.11 = (f32[16,1152]{1,0:T(8,128)}, f32[16,1152]{1,0:T(8,128)S(1)}, u32[]{:S(2)}) copy-start(f32[16,1152]{1,0:T(8,128)S(1)} %get-tuple-element.19.stat) | copy-start | bytes 221188
  57.2 20.9 %all-to-all-start.2 = ((f16[8,144,256]{2,1,0:T(8,128)(2,1)}), f16[8,144,256]{2,1,0:T(8,128)(2,1)}, u32[]{:S(2)}, u32[]{:S(2)}) async-start(f16[8,144,256]{2,1,0:T(8,128)(2,1)} %pad_maximum_fusion.1), calls=%async_computation.2 | async-start | bytes 1179648 | tf_op jit(solution)/shard_map/all_to_all | solution.py:156
  62.5 1.1 copy-start.10
  63.5 7.4 %copy-start.3 = (bf16[1024,128]{1,0:T(8,128)(2,1)S(1)}, bf16[1024,128]{1,0:T(8,128)(2,1)}, u32[]{:S(2)}) copy-start(bf16[1024,128]{1,0:T(8,128)(2,1)} %qr.5) | copy-start | bytes 786436
  63.5 7.4 %copy-start.5 = (bf16[1024,128]{1,0:T(8,128)(2,1)S(1)}, bf16[1024,128]{1,0:T(8,128)(2,1)}, u32[]{:S(2)}) copy-start(bf16[1024,128]{1,0:T(8,128)(2,1)} %gr.5) | copy-start | bytes 786436
  63.5 7.4 %copy-start.8 = (bf16[128,128]{1,0:T(8,128)(2,1)S(1)}, bf16[128,128]{1,0:T(8,128)(2,1)}, u32[]{:S(2)}) copy-start(bf16[128,128]{1,0:T(8,128)(2,1)} %gp.5) | copy-start | bytes 98308
  70.9 7.2 %collective-permute-start.1 = (f32[2048,256]{1,0:T(8,128)}, f32[2048,256]{1,0:T(8,128)}, u32[]{:S(2)}, u32[]{:S(2)}) collective-permute-start(f32[2048,256]{1,0:T(8,128)} %get-tuple-element.23), channel_id=1, source_target_pairs={{0,8},{8,0},{1,9},{9,1},{2,10},{10,2},{3,11},{11,3},{4,12},{12,4},... | collective-permute-start | bytes 6291464 | tf_op jit(solution)/shard_map/ppermute | solution.py:155
  71.0 0.9 copy-start.12
  81.7 25.0 %all-to-all-start.3 = ((f16[16,144,256]{2,1,0:T(8,128)(2,1)}), f16[16,144,256]{2,1,0:T(8,128)(2,1)S(1)}, u32[]{:S(2)}, u32[]{:S(2)}) async-start(f16[16,144,256]{2,1,0:T(8,128)(2,1)} %pad_maximum_fusion), calls=%async_computation.3 | async-start | bytes 2359296 | tf_op jit(solution)/shard_map/all_to_all | solution.py:156
  107.6 12.4 %all-to-all-start.4 = ((f32[8,16,256]{2,1,0:T(8,128)}), f32[8,16,256]{2,1,0:T(8,128)S(1)}, u32[]{:S(2)}, u32[]{:S(2)}) async-start(f32[8,16,256]{2,1,0:T(8,128)} %bitcast.2), calls=%async_computation.4 | async-start | bytes 262144 | tf_op jit(solution)/shard_map/all_to_all | solution.py:156
  120.9 12.9 %all-to-all-start.5 = ((bf16[8,144,256]{2,1,0:T(8,128)(2,1)}), bf16[8,144,256]{2,1,0:T(8,128)(2,1)S(1)}, u32[]{:S(2)}, u32[]{:S(2)}) async-start(bf16[8,144,256]{2,1,0:T(8,128)(2,1)} %broadcast_in_dim.24), calls=%async_computation.5 | async-start | bytes 1179648 | tf_op jit(solution)/shard_map/all_to_all | solution.py:156

commit v4 on v3

v4 whole, which is shorter than its diff:
```python
import functools, math
import jax, jax.numpy as jnp
from jax import lax
from jax.experimental import pallas as pl
from jax.experimental.pallas import tpu as pltpu
f32=jnp.float32; bf16=jnp.bfloat16
D=128
SCALE=1.0/math.sqrt(D)
RATE=math.log2(math.e)*SCALE
FAR=1e30
OWN=256
SEQ=("x_hi","z","core")
HEAD=("y","x_lo")
PLANE=("x_hi","y","x_lo")
LONG=8
HEADS=8
LINES=4
TILE=8
CORE_CHIPS=16
ROWS=16

def dot(a,b): return jnp.dot(a,b,preferred_element_type=f32)
def flip(x): return x.astype(f32).T.astype(bf16)
def fold(x): return x.reshape(x.shape[0]//8,8,x.shape[1])
def rows(i,n): return pl.ds(i*n,n)
def loop(n,step,init):
    for i in range(n): init=step(i,init)
    return init

def key_place(core,start,n,share,strip):
    r=start+lax.broadcasted_iota(jnp.int32,(n,share),0)
    wide=lambda size: size.bit_length()-1
    x=r>>wide(strip*CORE_CHIPS//2); head=(r>>wide(strip))&(HEADS-1); z=(r>>wide(ROWS))&(LONG-1); t=r&(ROWS-1)
    return ((x*LONG+z)*2+core)*share+head*ROWS+t

def pack(ref,b,cols,x):
    n=x.shape[0]
    power=jnp.ceil(jnp.log2(jnp.maximum(jnp.max(jnp.abs(x),axis=0,keepdims=True),2.0**-100)))
    ref[*b,:n,cols]=x*jnp.exp2(-power)
    ref[*b,n:,cols]=jnp.broadcast_to(power,(TILE,x.shape[1]))

KEYS,VALUES=slice(0,D),slice(D,2*D)

def seq_place():
    return (lax.axis_index(SEQ[0])*LONG+lax.axis_index(SEQ[1]))*2+lax.axis_index(SEQ[2])

def forward(KC,info,qp,gp,near,far,qr,gr,kvr,op,our,carry,own2,s,own):
    length=info[0]; first=seq_place()*qp.shape[0]
    core=lax.axis_index("core")
    half=near.shape[0]; count=2*half; span=qr.shape[0]; share=qp.shape[0]; n=span+share
    qt=jnp.concatenate([flip(qr[...]),flip(qp[...])],axis=1)
    gt=jnp.concatenate([flip(gr[...]),flip(gp[...])],axis=1)
    def part(i):
        return (near if i*KC<half else far)[pl.ds(i*KC%half,KC),:]
    def seen(i):
        place=key_place(core if i*KC<half else 1-core,i*KC%half,KC,share,half//CORE_CHIPS)
        return place<=first+lax.broadcasted_iota(jnp.int32,(KC,share),1)
    tri=lax.broadcasted_iota(jnp.int32,(OWN,OWN),0)<=lax.broadcasted_iota(jnp.int32,(OWN,OWN),1)
    def top(i,m):
        x=dot(part(i)[:,:D],qt)
        x=jnp.concatenate([x[:,:span],jnp.where(seen(i),x[:,span:],-FAR)],axis=1)
        s[rows(i,KC),:]=x
        return jnp.maximum(m,jnp.max(fold(x),axis=0))
    m=loop(count//KC,top,jnp.full((8,n),-FAR,f32))
    mr=m[:,:span]
    for j in range(span//OWN):
        x=dot(kvr[j*OWN:(j+1)*OWN,:D],qt[:,j*OWN:span])
        d=jnp.where(tri,x[:,:OWN],-FAR)
        x=d if x.shape[1]==OWN else jnp.concatenate([d,x[:,OWN:]],axis=1)
        own[j*OWN:(j+1)*OWN,j*OWN:span]=x
        y=jnp.max(fold(x),axis=0)
        y=jnp.maximum(mr[:,j*OWN:],y)
        mr=y if j==0 else jnp.concatenate([mr[:,:j*OWN],y],axis=1)
    m=jnp.max(jnp.concatenate([mr,m[:,span:]],axis=1),axis=0,keepdims=True)*RATE
    def total(i,l):
        e=jnp.exp2(s[rows(i,KC),:]*RATE-m)
        s[rows(i,KC),:]=e
        return l+jnp.sum(fold(e),axis=0)
    l=loop(count//KC,total,jnp.zeros((8,n),f32))
    lr=l[:,:span]
    for j in range(span//OWN):
        y=lr[:,j*OWN:]+jnp.sum(fold(jnp.exp2(own[j*OWN:(j+1)*OWN,j*OWN:span]*RATE-m[:,j*OWN:span])),axis=0)
        lr=y if j==0 else jnp.concatenate([lr[:,:j*OWN],y],axis=1)
    l=jnp.sum(jnp.concatenate([lr,l[:,span:]],axis=1),axis=0,keepdims=True)
    level=m+jnp.log2(l)
    at=lax.broadcasted_iota(jnp.int32,(1,n),1)
    live=(at<length)|(at>=span)
    inv=jnp.where(live,1.0/l,0.0)
    level=jnp.where(live,level,FAR)
    def attend(i,o):
        p=(s[rows(i,KC),:]*inv).astype(bf16)
        return o+dot(flip(part(i)[:,D:]),p)
    o=loop(count//KC,attend,jnp.zeros((D,n),f32))
    tail=o[:,span:]
    o=o[:,:span]
    for j in range(span//OWN):
        p=jnp.exp2(own[j*OWN:(j+1)*OWN,j*OWN:span]*RATE-level[:,j*OWN:span]).astype(bf16)
        y=o[:,j*OWN:]+dot(flip(kvr[j*OWN:(j+1)*OWN,D:]),p)
        o=y if j==0 else jnp.concatenate([o[:,:j*OWN],y],axis=1)
    our[...]=o.T.astype(bf16)
    op[...]=tail.T.astype(bf16)
    delta=jnp.sum(gt.astype(f32)*jnp.concatenate([o,tail],axis=1),axis=0,keepdims=True)
    carry[D:D+8,:]=jnp.broadcast_to(level,(8,n))
    carry[D+8:,:]=jnp.broadcast_to(delta,(8,n))
    dq=jnp.zeros((D,span),f32)
    for j in range(span//OWN):
        a=slice(j*OWN,(j+1)*OWN); b=slice(j*OWN,span)
        p=jnp.exp2(own[a,b]*RATE-level[:,b])
        dp=dot(kvr[a,D:],gt[:,b])
        ds=(p*(dp-delta[:,b])).astype(bf16)
        dv=dot(p.astype(bf16),gr[b,:])
        dk=dot(ds,qr[b,:])*SCALE
        strip=span//HEADS
        for t in range(OWN//strip):
            u=slice(t*strip,(t+1)*strip)
            x,y=divmod(j*(OWN//strip)+t,LINES)
            at=(x^lax.axis_index("x_lo"),(y-lax.axis_index("y"))&(LINES-1))
            pack(own2,at,VALUES,dv[u])
            pack(own2,at,KEYS,dk[u])
        y=dq[:,b]+dot(flip(kvr[a,:D]),ds)
        dq=y if j==0 else jnp.concatenate([dq[:,:j*OWN],y],axis=1)
    carry[:D,:]=jnp.concatenate([dq,jnp.zeros((D,share),f32)],axis=1)

def half_block(kv): return kv.shape[0]//CORE_CHIPS

def backward(KC,last,qp,gp,kv,qr,gr,carry,*out):
    if last: other,*out=out
    *out,grad=out
    block=half_block(kv)
    first=seq_place()*qp.shape[0]
    core=lax.axis_index("core")
    if not last: core=1-core
    half=kv.shape[0]; span=qr.shape[0]; share=qp.shape[0]
    qt=jnp.concatenate([flip(qr[...]),flip(qp[...])],axis=1)
    gt=jnp.concatenate([flip(gr[...]),flip(gp[...])],axis=1)
    q=jnp.concatenate([qr[...],qp[...]],axis=0)
    g=jnp.concatenate([gr[...],gp[...]],axis=0)
    level=carry[D:D+1,:]; delta=carry[D+8:D+9,:]
    def seen(i):
        place=key_place(core,i*KC,KC,share,half//CORE_CHIPS)
        return place<=first+lax.broadcasted_iota(jnp.int32,(KC,share),1)
    def step(i,dq):
        a=rows(i,KC)
        x=dot(kv[a,:D],qt)
        dp=dot(kv[a,D:],gt)
        p=jnp.exp2(x*RATE-level)
        p=jnp.concatenate([p[:,:span],jnp.where(seen(i),p[:,span:],0.0)],axis=1)
        ds=(p*(dp-delta)).astype(bf16)
        dv=dot(p.astype(bf16),g)
        dk=dot(ds,q)*SCALE
        if last:
            dv=dv+other[a,D:]
            dk=dk+other[a,:D]
            for t in range(KC//block):
                u=slice(t*block,(t+1)*block)
                pack(grad,(i*(KC//block)+t,),VALUES,dv[u])
                pack(grad,(i*(KC//block)+t,),KEYS,dk[u])
        else:
            grad[a,D:]=dv
            grad[a,:D]=dk
        return dq+dot(flip(kv[a,:D]),ds)
    dq=loop(half//KC,step,carry[:D,:])
    if not last:
        out[0][:D,:]=dq
        out[0][D:,:]=carry[D:,:]
    else:
        dq=(dq*SCALE).T.astype(bf16)
        out[0][...]=dq[:span]
        out[1][...]=dq[span:]

V=pl.BlockSpec(memory_space=pltpu.VMEM)
SM=pl.BlockSpec(memory_space=pltpu.SMEM)
def shape(s,t=f32): return jax.ShapeDtypeStruct(s,t)

def run_forward(lengths,qp,gp,near,far,qr,gr,kvr,KC=512):
    span=qr.shape[0]; half=near.shape[0]; share=qp.shape[0]; n=span+share
    return pl.pallas_call(functools.partial(forward,KC),
        out_shape=(shape(qp.shape,bf16),shape(qr.shape,bf16),shape((D+16,n)),shape((2,LINES,span//HEADS+TILE,2*D))),
        in_specs=[SM]+[V]*7,out_specs=(V,)*4,
        scratch_shapes=[pltpu.VMEM((2*half,n),f32),pltpu.VMEM((span,span),f32)],
        cost_estimate=pl.CostEstimate(flops=5*n*half*2*D,bytes_accessed=2**23,transcendentals=4*n*half),
        compiler_params=pltpu.CompilerParams(vmem_limit_bytes=46*1024*1024),name="forward")(lengths,qp,gp,near,far,qr,gr,kvr)

def run_backward(last,qp,gp,kv,qr,gr,carry,*other,KC=512):
    n=carry.shape[1]; half=kv.shape[0]
    return pl.pallas_call(functools.partial(backward,KC,last),
        out_shape=((shape(qr.shape,bf16),shape(qp.shape,bf16)) if last else (shape(carry.shape),))+(shape((CORE_CHIPS,half_block(kv)+TILE,2*D)) if last else shape(kv.shape),),
        in_specs=[V]*(6+last),out_specs=(V,)*(2+last),
        cost_estimate=pl.CostEstimate(flops=50*n*half*2*D,bytes_accessed=2**22,transcendentals=n*half),
        compiler_params=pltpu.CompilerParams(vmem_limit_bytes=28*1024*1024),name="backward")(qp,gp,kv,qr,gr,carry,*other)

def swap(x): return lax.ppermute(x,"core",[(0,1),(1,0)])
def spread(x,axes): return lax.all_to_all(x,axes,0,0,tiled=True)
def copies(x,n): return jnp.broadcast_to(x[None],(n,)+x.shape)

def unpack(x):
    rest=jnp.exp2(x[:,-TILE:].astype(f32))
    x=x[:,:-TILE].astype(f32).reshape(x.shape[0],-1,TILE,x.shape[2])
    return x*rest[:,None]

def turn(x,by): return lax.ppermute(x,"y",[(i,(i+by)%LINES) for i in range(LINES)])

def on_device(qp,kvp,qr,kvr,gp,gr,lengths):
    head=lax.axis_index(HEAD)
    piece=lax.dynamic_slice_in_dim(kvp,head*ROWS,ROWS,0)
    line=spread(copies(piece,LONG),"z").reshape(-1,2*D)
    near=spread(copies(line,CORE_CHIPS),PLANE).reshape(-1,2*D)
    far=swap(near)
    op,our,carry,own=run_forward(lengths,qp,gp,near,far,qr,gr,kvr)
    met=lax.ppermute(own[1].astype(jnp.float16),"x_lo",[(0,1),(1,0)])
    carry,dfar=run_backward(False,qp,gp,far,qr,gr,carry)
    carry,dfar,met=lax.optimization_barrier((carry,dfar,met))
    own=(unpack(own[0])+unpack(met)).reshape(LINES,-1,2*D)
    turns=[turn(own[i],i) for i in range(1,LINES)]
    dqr,dqp,chip=run_backward(True,qp,gp,near,qr,gr,carry,swap(dfar))
    chip,turns=lax.optimization_barrier((chip,turns))
    chip,own=lax.optimization_barrier((chip.astype(jnp.float16),own[0]+turns[0]+turns[1]+turns[2]))
    line=unpack(spread(chip,PLANE)).sum(0)
    strip=spread(line.reshape(LONG,ROWS,2*D),"z").sum(0)
    done=jnp.concatenate([strip,own]).astype(bf16)
    done=spread(copies(done,HEADS),HEAD)
    mine=done[:,ROWS:].reshape(LINES,2,-1,2*D).transpose(1,0,2,3).reshape(-1,2*D)
    return (op,our,dqp,dqr,done[:,:ROWS].reshape(-1,2*D),mine)

def solution(mesh):
    P=jax.sharding.PartitionSpec
    fine=jax.sharding.Mesh(mesh.devices.reshape(2,LONG,2,4,2),SEQ+HEAD)
    rows_,cache=P(SEQ,HEAD),P(SEQ,None)
    return jax.shard_map(on_device,mesh=fine,
        in_specs=(rows_,cache,rows_,cache,rows_,rows_,P(SEQ)),
        out_specs=(rows_,rows_,rows_,rows_,cache,cache),check_vma=False)
```

time: 136 us -> 123 us (0.904)
  blocking collectives: 38.8 us -> 83.5 us
  waiting for transfers between devices: 35.1 us -> 4.01 us
  starting transfers between devices: 19.1 us -> 4.75 us
  other arithmetic: 7.78 us -> 0.69 us
  local copies, waits for them, and re-layouts: 6.96 us -> 2.47 us
    all_to_all x2 -> x5, blocking collectives: 38.8 us -> 83.5 us  [spread(): return lax.all_to_all(x, axes, 0, 0, tiled=True)]
    all_to_all x4 -> x0, waiting for transfers between devices: 33.1 us -> none  [spread(): return lax.all_to_all(x, axes, 0, 0, tiled=True)]
    all_to_all x4 -> x0, starting transfers between devices: 19 us -> none  [spread(): return lax.all_to_all(x, axes, 0, 0, tiled=True)]
    ppermute x0 -> x4, starting transfers between devices: none -> 4.75 us  [the longest x3 3.31 us: turn(): return lax.ppermute(x, 'y', [(i, (i + by) % LINES) for i in range(LINES)])]
    unnamed x28 -> x12, local copies, waits for them, and re-layouts: 3.16 us -> 0.8 us
    concatenate x2 -> x1, other arithmetic: 2.27 us -> 0.01 us  [on_device(): done = jnp.concatenate([strip, own]).astype(bf16)]
    slice x4 -> x2, local copies, waits for them, and re-layouts: 2.8 us -> 0.67 us  [the longest x1 0.63 us: on_device(): return (op, our, dqp, dqr, done[:, :ROWS].reshape(-1, 2 * D), mine)]
    reduce_max x2 -> x0, other arithmetic: 1.98 us -> none  [pack(): top = jnp.maximum(jnp.max(jnp.abs(x), axis=1, keepdims=True), 2.0 ** (-100))]
  transfers between devices with their start and end apart: 6 -> 6, of which waited for: 4 -> 3; matrix products, arithmetic and copies ran while one was open for 2% -> 0% of each run, Pallas kernels for 10% -> 11%
where the time goes in v4:
time: 123 us; the launch traced here: 122 us
  blocking collectives  83.5 us (68%)
  Pallas kernels  25.4 us (21%)
  starting transfers between devices  4.75 us (4%)
  waiting for transfers between devices  4.01 us (3%)
  local copies, waits for them, and re-layouts  2.47 us (2%)
  between operations  1.46 us (1%)
    all_to_all x5, blocking collectives, spread(): return lax.all_to_all(x, axes, 0, 0, tiled=True)  83.5 us
    pallas_call x2, Pallas kernels, run_backward(): pl.pallas_call(functools.partial(backward, KC, last), out_shape=((shape(q...  13.7 us
    pallas_call x1, Pallas kernels, run_forward(): pl.pallas_call(functools.partial(forward, KC), out_shape=(shape(qp.shape,...  11.8 us
    ppermute x3, starting transfers between devices, turn(): return lax.ppermute(x, 'y', [(i, (i + by) % LINES) for i in range(LINES)])  3.31 us
    ppermute x2, waiting for transfers between devices, swap(): return lax.ppermute(x, 'core', [(0, 1), (1, 0)])  2.69 us
  transfers between devices with their start and end apart: 6, of which 3 were waited for; matrix products, arithmetic and copies ran while one was open for 0% of the time, Pallas kernels for 11%

profile of v4, /device:TPU:2, one launch (start us, length us, event | category | flops | bytes accessed | tf_op | source)
XLA Modules:
  0.0 122.4 jit_solution(17085393417888547515)
XLA Ops:
  0.6 0.0 copy-start
  0.6 0.0 copy-start.4
  0.7 0.0 copy-start.5
  0.7 0.8 copy-done
  1.5 16.6 %all_to_all.25 = bf16[8,16,256]{2,1,0:T(8,128)(2,1)S(1)} all-to-all(bf16[8,16,256]{2,1,0:T(8,128)(2,1)S(1)} %broadcast_in_dim.8), channel_id=1, replica_groups=mesh['x_hi'=2,'z'=8,'core'=2,'y'=4,'x_lo'=2] {'z'}, dimensions={0} | all-to-all | bytes 131072 | tf_op jit(solution)/shard_map/all_to_all | solution.py:193
  18.1 0.1 broadcast_in_dim.10
  18.2 22.2 %all_to_all.26 = bf16[16,128,256]{2,1,0:T(8,128)(2,1)S(1)} all-to-all(bf16[16,128,256]{2,1,0:T(8,128)(2,1)S(1)} %broadcast_in_dim.10), channel_id=1, replica_groups=mesh['x_hi'=2,'z'=8,'core'=2,'y'=4,'x_lo'=2] {'x_hi','y','x_lo'}, dimensions={0} | all-to-all | bytes 2097152 | tf_op jit(solution)/shard_map/all_to_all | solution.py:193
  40.4 0.0 collective-permute-start
  41.1 2.0 %collective-permute-done.far.kv = bf16[2048,256]{1,0:T(8,128)(2,1)S(1)} collective-permute-done((bf16[2048,256]{1,0:T(8,128)(2,1)S(1)}, bf16[2048,256]{1,0:T(8,128)(2,1)S(1)}, u32[]{:S(2)}, u32[]{:S(2)}) %collective-permute-start) | collective-permute-done | bytes 1048608 | tf_op jit(solution)/shard_map/ppermute | solution.py:192
  43.1 0.0 copy-done.5
  43.1 11.8 %forward.1 = (bf16[128,128]{1,0:T(8,128)(2,1)}, bf16[1024,128]{1,0:T(8,128)(2,1)}, f32[144,1152]{1,0:T(8,128)S(1)}, f32[2,4,136,256]{3,2,1,0:T(8,128)S(1)}) custom-call(s32[1]{0:T(128)S(6)} %copy.15.info, bf16[128,128]{1,0:T(8,128)(2,1)S(1)} %copy-done.4, bf16[128,128]{1,0:T(8,128)(2,1)S(1)} %copy-done.5, bf16[2048,256]{1,0:T(8,128)(2,1)S(1)} %bitcast.40, ...), custom_call_target="tpu_custom_call" | custom-call | flops 3019898880 | bytes 8388608 | tf_op jit(solution)/shard_map/forward/pallas_call | solution.py:177
  54.9 0.1 slice_bitcast_fusion
  55.0 1.4 %collective-permute-start.1 = (f16[4,136,256]{2,1,0:T(8,128)(2,1)S(1)}, f16[4,136,256]{2,1,0:T(8,128)(2,1)S(1)}, u32[]{:S(2)}, u32[]{:S(2)}) collective-permute-start(f16[4,136,256]{2,1,0:T(8,128)(2,1)S(1)} %get-tuple-element.43), channel_id=1, source_target_pairs={{0,1},{1,0},{2,3},{3,2},{4,5},{5,4},{6,7},{7,6},{8,9},{9,8},{10,11... | collective-permute-start | bytes 835592 | tf_op jit(solution)/shard_map/ppermute | solution.py:210
  56.4 6.2 %backward.2 = (f32[144,1152]{1,0:T(8,128)S(1)}, f32[2048,256]{1,0:T(8,128)S(1)}) custom-call(bf16[128,128]{1,0:T(8,128)(2,1)S(1)} %copy-done.4, bf16[128,128]{1,0:T(8,128)(2,1)S(1)} %copy-done.5, bf16[2048,256]{1,0:T(8,128)(2,1)S(1)} %collective-permute-done.far.kv, bf16[1024,128]{1,0:T(8,128)(2,1)S(1)} %copy-done.2, bf16[1024,128]{1,0:T(8,128)(2,1)S(1)} %copy-done.3, ...), custom_call_target="tpu_custom_call" | custom-call | flops 30198988800 | bytes 4194304 | tf_op jit(solution)/shard_map/backward/pallas_call | solution.py:186
  62.6 1.3 %collective-permute-done.1 = f16[4,136,256]{2,1,0:T(8,128)(2,1)S(1)} collective-permute-done((f16[4,136,256]{2,1,0:T(8,128)(2,1)S(1)}, f16[4,136,256]{2,1,0:T(8,128)(2,1)S(1)}, u32[]{:S(2)}, u32[]{:S(2)}) %collective-permute-start.1) | collective-permute-done | bytes 278560 | tf_op jit(solution)/shard_map/ppermute | solution.py:210
  63.9 0.0 collective-permute-start.2
  64.0 0.1 fusion.2
  64.1 0.1 collective-permute-start.3
  64.2 2.1 %collective-permute-start.4 = (f32[128,256]{1,0:T(8,128)S(1)}, f32[128,256]{1,0:T(8,128)S(1)}, u32[]{:S(2)}, u32[]{:S(2)}) collective-permute-start(f32[128,256]{1,0:T(8,128)S(1)} %get-tuple-element.45), channel_id=1, source_target_pairs={{0,4},{2,6},{4,0},{6,2},{1,5},{3,7},{5,1},{7,3},{8,12},{10,14},{12... | collective-permute-start | bytes 393224 | tf_op jit(solution)/shard_map/ppermute | solution.py:201
  66.2 1.2 collective-permute-start.5
  67.4 0.7 collective-permute-done.2.out_0_
  68.1 7.5 %backward.3 = (bf16[1024,128]{1,0:T(8,128)(2,1)}, bf16[128,128]{1,0:T(8,128)(2,1)}, f32[16,136,256]{2,1,0:T(8,128)S(1)}) custom-call(bf16[128,128]{1,0:T(8,128)(2,1)S(1)} %copy-done.4, bf16[128,128]{1,0:T(8,128)(2,1)S(1)} %copy-done.5, bf16[2048,256]{1,0:T(8,128)(2,1)S(1)} %bitcast.41, bf16[1024,128]{1,0:T(8,128)(2,1)S(1)} %copy-done.2, ...), custom_call_target="tpu_custom_call" | custom-call | flops 30198988800 | bytes 4194304 | tf_op jit(solution)/shard_map/backward/pallas_call | solution.py:186
  75.5 0.0 collective-permute-done.3
  75.5 0.0 collective-permute-done.4
  75.5 0.0 collective-permute-done.5
  75.5 0.2 convert_element_type.24
  75.8 21.5 %all_to_all.27 = f16[16,136,256]{2,1,0:T(8,128)(2,1)S(1)} all-to-all(f16[16,136,256]{2,1,0:T(8,128)(2,1)S(1)} %convert_element_type.24), channel_id=1, replica_groups=mesh['x_hi'=2,'z'=8,'core'=2,'y'=4,'x_lo'=2] {'x_hi','y','x_lo'}, dimensions={0} | all-to-all | bytes 2228224 | tf_op jit(solution)/shard_map/all_to_all | solution.py:193
  97.4 0.2 fusion
  97.6 11.5 %all_to_all.28 = f32[8,16,256]{2,1,0:T(8,128)S(1)} all-to-all(f32[8,16,256]{2,1,0:T(8,128)S(1)} %bitcast.43), channel_id=1, replica_groups=mesh['x_hi'=2,'z'=8,'core'=2,'y'=4,'x_lo'=2] {'z'}, dimensions={0} | all-to-all | bytes 262144 | tf_op jit(solution)/shard_map/all_to_all | solution.py:193
  109.1 11.7 %all_to_all.29 = bf16[8,144,256]{2,1,0:T(8,128)(2,1)S(1)} all-to-all(bf16[8,144,256]{2,1,0:T(8,128)(2,1)S(1)} %broadcast_in_dim.11), channel_id=1, replica_groups=mesh['x_hi'=2,'z'=8,'core'=2,'y'=4,'x_lo'=2] {'y','x_lo'}, dimensions={0} | all-to-all | bytes 1179648 | tf_op jit(solution)/shard_map/all_to_all | solution.py:193
  120.9 0.8 copy.14
  121.7 0.6 slice.70
  (18 shorter events, 0.2 us)
Async XLA Ops:
  0.6 0.8 copy-start
  0.6 42.4 %copy-start.4 = (bf16[128,128]{1,0:T(8,128)(2,1)S(1)}, bf16[128,128]{1,0:T(8,128)(2,1)}, u32[]{:S(2)}) copy-start(bf16[128,128]{1,0:T(8,128)(2,1)} %qp.5) | copy-start | bytes 98308
  0.7 42.4 %copy-start.5 = (bf16[128,128]{1,0:T(8,128)(2,1)S(1)}, bf16[128,128]{1,0:T(8,128)(2,1)}, u32[]{:S(2)}) copy-start(bf16[128,128]{1,0:T(8,128)(2,1)} %gp.5) | copy-start | bytes 98308
  0.7 42.4 %copy-start.2 = (bf16[1024,128]{1,0:T(8,128)(2,1)S(1)}, bf16[1024,128]{1,0:T(8,128)(2,1)}, u32[]{:S(2)}) copy-start(bf16[1024,128]{1,0:T(8,128)(2,1)} %qr.5) | copy-start | bytes 786436
  0.7 42.4 %copy-start.3 = (bf16[1024,128]{1,0:T(8,128)(2,1)S(1)}, bf16[1024,128]{1,0:T(8,128)(2,1)}, u32[]{:S(2)}) copy-start(bf16[1024,128]{1,0:T(8,128)(2,1)} %gr.5) | copy-start | bytes 786436
  0.7 42.4 %copy-start.1 = (bf16[1024,256]{1,0:T(8,128)(2,1)S(1)}, bf16[1024,256]{1,0:T(8,128)(2,1)}, u32[]{:S(2)}) copy-start(bf16[1024,256]{1,0:T(8,128)(2,1)} %kvr.1) | copy-start | bytes 1572868
  40.4 2.7 %collective-permute-start = (bf16[2048,256]{1,0:T(8,128)(2,1)S(1)}, bf16[2048,256]{1,0:T(8,128)(2,1)S(1)}, u32[]{:S(2)}, u32[]{:S(2)}) collective-permute-start(bf16[2048,256]{1,0:T(8,128)(2,1)S(1)} %bitcast.39), channel_id=1, source_target_pairs={{0,8},{8,0},{1,9},{9,1},{2,10},{10,2},{3,11},{11,3},{4,12},{12,4},... | collective-permute-start | bytes 3145736 | tf_op jit(solution)/shard_map/ppermute | solution.py:192
  55.0 9.0 %collective-permute-start.1 = (f16[4,136,256]{2,1,0:T(8,128)(2,1)S(1)}, f16[4,136,256]{2,1,0:T(8,128)(2,1)S(1)}, u32[]{:S(2)}, u32[]{:S(2)}) collective-permute-start(f16[4,136,256]{2,1,0:T(8,128)(2,1)S(1)} %get-tuple-element.43), channel_id=1, source_target_pairs={{0,1},{1,0},{2,3},{3,2},{4,5},{5,4},{6,7},{7,6},{8,9},{9,8},{10,11... | collective-permute-start | bytes 835592 | tf_op jit(solution)/shard_map/ppermute | solution.py:210
  63.9 4.2 %collective-permute-start.2 = (f32[2048,256]{1,0:T(8,128)S(1)}, f32[2048,256]{1,0:T(8,128)S(1)}, u32[]{:S(2)}, u32[]{:S(2)}) collective-permute-start(f32[2048,256]{1,0:T(8,128)S(1)} %get-tuple-element.31), channel_id=1, source_target_pairs={{0,8},{8,0},{1,9},{9,1},{2,10},{10,2},{3,11},{11,3},{4,12},{12,4},... | collective-permute-start | bytes 6291464 | tf_op jit(solution)/shard_map/ppermute | solution.py:192
  64.1 11.5 %collective-permute-start.3 = (f32[128,256]{1,0:T(8,128)S(1)}, f32[128,256]{1,0:T(8,128)S(1)}, u32[]{:S(2)}, u32[]{:S(2)}) collective-permute-start(f32[128,256]{1,0:T(8,128)S(1)} %get-tuple-element.46), channel_id=1, source_target_pairs={{0,2},{2,4},{4,6},{6,0},{1,3},{3,5},{5,7},{7,1},{8,10},{10,12},{12... | collective-permute-start | bytes 393224 | tf_op jit(solution)/shard_map/ppermute | solution.py:201
  64.2 11.4 %collective-permute-start.4 = (f32[128,256]{1,0:T(8,128)S(1)}, f32[128,256]{1,0:T(8,128)S(1)}, u32[]{:S(2)}, u32[]{:S(2)}) collective-permute-start(f32[128,256]{1,0:T(8,128)S(1)} %get-tuple-element.45), channel_id=1, source_target_pairs={{0,4},{2,6},{4,0},{6,2},{1,5},{3,7},{5,1},{7,3},{8,12},{10,14},{12... | collective-permute-start | bytes 393224 | tf_op jit(solution)/shard_map/ppermute | solution.py:201
  66.2 9.3 %collective-permute-start.5 = (f32[128,256]{1,0:T(8,128)S(1)}, f32[128,256]{1,0:T(8,128)S(1)}, u32[]{:S(2)}, u32[]{:S(2)}) collective-permute-start(f32[128,256]{1,0:T(8,128)S(1)} %get-tuple-element.44), channel_id=1, source_target_pairs={{0,6},{2,0},{4,2},{6,4},{1,7},{3,1},{5,3},{7,5},{8,14},{10,8},{12,... | collective-permute-start | bytes 393224 | tf_op jit(solution)/shard_map/ppermute | solution.py:201

commit v5 on v4

v5 whole, which is shorter than its diff:
```python
import functools, math
import jax, jax.numpy as jnp
from jax import lax
from jax.experimental import pallas as pl
from jax.experimental.pallas import tpu as pltpu
f32=jnp.float32; bf16=jnp.bfloat16
D=128
SCALE=1.0/math.sqrt(D)
RATE=math.log2(math.e)*SCALE
FAR=1e30
OWN=256
SEQ=("x_hi","z","core")
HEAD=("y","x_lo")
PLANE=("x_hi","y","x_lo")
LONG=8
HEADS=8
LINES=4
TILE=8
CORE_CHIPS=16
ROWS=16

def dot(a,b): return jnp.dot(a,b,preferred_element_type=f32)
def flip(x): return x.astype(f32).T.astype(bf16)
def fold(x): return x.reshape(x.shape[0]//8,8,x.shape[1])
def rows(i,n): return pl.ds(i*n,n)
def loop(n,step,init):
    for i in range(n): init=step(i,init)
    return init

def key_place(core,start,n,share,strip):
    r=start+lax.broadcasted_iota(jnp.int32,(n,share),0)
    wide=lambda size: size.bit_length()-1
    x=r>>wide(strip*CORE_CHIPS//2); head=(r>>wide(strip))&(HEADS-1); z=(r>>wide(ROWS))&(LONG-1); t=r&(ROWS-1)
    return ((x*LONG+z)*2+core)*share+head*ROWS+t

def pack(ref,b,cols,x):
    n=x.shape[0]
    power=jnp.ceil(jnp.log2(jnp.maximum(jnp.max(jnp.abs(x),axis=0,keepdims=True),2.0**-100)))
    ref[*b,:n,cols]=x*jnp.exp2(-power)
    ref[*b,n:,cols]=jnp.broadcast_to(power,(TILE,x.shape[1]))

KEYS,VALUES=slice(0,D),slice(D,2*D)

def seq_place():
    return (lax.axis_index(SEQ[0])*LONG+lax.axis_index(SEQ[1]))*2+lax.axis_index(SEQ[2])

def forward(KC,info,qp,gp,near,far,qr,gr,kvr,op,our,carry,own2,enear,efar,own):
    length=info[0]; first=seq_place()*qp.shape[0]
    core=lax.axis_index("core")
    half=near.shape[0]; count=2*half; span=qr.shape[0]; share=qp.shape[0]; n=span+share
    qt=jnp.concatenate([flip(qr[...]),flip(qp[...])],axis=1)
    gt=jnp.concatenate([flip(gr[...]),flip(gp[...])],axis=1)
    def part(i):
        return (near if i*KC<half else far)[pl.ds(i*KC%half,KC),:]
    def scores(i):
        return (enear if i*KC<half else efar).at[pl.ds(i*KC%half,KC),:]
    def seen(i):
        place=key_place(core if i*KC<half else 1-core,i*KC%half,KC,share,half//CORE_CHIPS)
        return place<=first+lax.broadcasted_iota(jnp.int32,(KC,share),1)
    tri=lax.broadcasted_iota(jnp.int32,(OWN,OWN),0)<=lax.broadcasted_iota(jnp.int32,(OWN,OWN),1)
    def top(i,m):
        x=dot(part(i)[:,:D],qt)
        x=jnp.concatenate([x[:,:span],jnp.where(seen(i),x[:,span:],-FAR)],axis=1)
        scores(i)[...]=x
        return jnp.maximum(m,jnp.max(fold(x),axis=0))
    m=loop(count//KC,top,jnp.full((8,n),-FAR,f32))
    mr=m[:,:span]
    for j in range(span//OWN):
        x=dot(kvr[j*OWN:(j+1)*OWN,:D],qt[:,j*OWN:span])
        d=jnp.where(tri,x[:,:OWN],-FAR)
        x=d if x.shape[1]==OWN else jnp.concatenate([d,x[:,OWN:]],axis=1)
        own[j*OWN:(j+1)*OWN,j*OWN:span]=x
        y=jnp.max(fold(x),axis=0)
        y=jnp.maximum(mr[:,j*OWN:],y)
        mr=y if j==0 else jnp.concatenate([mr[:,:j*OWN],y],axis=1)
    m=jnp.max(jnp.concatenate([mr,m[:,span:]],axis=1),axis=0,keepdims=True)
    def total(i,l):
        e=jnp.exp2((scores(i)[...]-m)*RATE)
        scores(i)[...]=e
        return l+jnp.sum(fold(e),axis=0)
    l=loop(count//KC,total,jnp.zeros((8,n),f32))
    lr=l[:,:span]
    for j in range(span//OWN):
        e=jnp.exp2((own[j*OWN:(j+1)*OWN,j*OWN:span]-m[:,j*OWN:span])*RATE)
        own[j*OWN:(j+1)*OWN,j*OWN:span]=e
        y=lr[:,j*OWN:]+jnp.sum(fold(e),axis=0)
        lr=y if j==0 else jnp.concatenate([lr[:,:j*OWN],y],axis=1)
    l=jnp.sum(jnp.concatenate([lr,l[:,span:]],axis=1),axis=0,keepdims=True)
    at=lax.broadcasted_iota(jnp.int32,(1,n),1)
    live=(at<length)|(at>=span)
    inv=jnp.where(live,1.0/l,0.0)
    def attend(i,o):
        p=(scores(i)[...]*inv).astype(bf16)
        return o+dot(flip(part(i)[:,D:]),p)
    o=loop(count//KC,attend,jnp.zeros((D,n),f32))
    tail=o[:,span:]
    o=o[:,:span]
    for j in range(span//OWN):
        p=(own[j*OWN:(j+1)*OWN,j*OWN:span]*inv[:,j*OWN:span]).astype(bf16)
        y=o[:,j*OWN:]+dot(flip(kvr[j*OWN:(j+1)*OWN,D:]),p)
        o=y if j==0 else jnp.concatenate([o[:,:j*OWN],y],axis=1)
    our[...]=o.T.astype(bf16)
    op[...]=tail.T.astype(bf16)
    delta=jnp.sum(gt.astype(f32)*jnp.concatenate([o,tail],axis=1),axis=0,keepdims=True)
    carry[D:D+8,:]=jnp.broadcast_to(inv,(8,n))
    carry[D+8:,:]=jnp.broadcast_to(delta,(8,n))
    dq=jnp.zeros((D,span),f32)
    for j in range(span//OWN):
        a=slice(j*OWN,(j+1)*OWN); b=slice(j*OWN,span)
        p=own[a,b]*inv[:,b]
        dp=dot(kvr[a,D:],gt[:,b])
        ds=(p*(dp-delta[:,b])).astype(bf16)
        dv=dot(p.astype(bf16),gr[b,:])
        dk=dot(ds,qr[b,:])*SCALE
        strip=span//HEADS
        for t in range(OWN//strip):
            u=slice(t*strip,(t+1)*strip)
            x,y=divmod(j*(OWN//strip)+t,LINES)
            at=((y-lax.axis_index("y"))&(LINES-1),x^lax.axis_index("x_lo"))
            pack(own2,at,VALUES,dv[u])
            pack(own2,at,KEYS,dk[u])
        y=dq[:,b]+dot(flip(kvr[a,:D]),ds)
        dq=y if j==0 else jnp.concatenate([dq[:,:j*OWN],y],axis=1)
    carry[:D,:]=jnp.concatenate([dq,jnp.zeros((D,share),f32)],axis=1)

def combine(mine,other,out):
    n=mine.shape[0]//CORE_CHIPS
    for b in range(CORE_CHIPS):
        x=mine[rows(b,n),:]+other[rows(b,n),:]
        pack(out,(b,),slice(0,2*D),x)

def backward(KC,last,qp,gp,kv,qr,gr,e,carry,*out):
    *out,grad=out
    half=kv.shape[0]; span=qr.shape[0]; share=qp.shape[0]
    gt=jnp.concatenate([flip(gr[...]),flip(gp[...])],axis=1)
    q=jnp.concatenate([qr[...],qp[...]],axis=0)
    g=jnp.concatenate([gr[...],gp[...]],axis=0)
    inv=carry[D:D+1,:]; delta=carry[D+8:D+9,:]
    def step(i,dq):
        a=rows(i,KC)
        dp=dot(kv[a,D:],gt)
        p=e[a,:]*inv
        ds=(p*(dp-delta)).astype(bf16)
        dv=dot(p.astype(bf16),g)
        dk=dot(ds,q)*SCALE
        grad[a,D:]=dv
        grad[a,:D]=dk
        return dq+dot(flip(kv[a,:D]),ds)
    dq=loop(half//KC,step,carry[:D,:])
    if not last:
        out[0][:D,:]=dq
        out[0][D:,:]=carry[D:,:]
    else:
        dq=(dq*SCALE).T.astype(bf16)
        out[0][...]=dq[:span]
        out[1][...]=dq[span:]

V=pl.BlockSpec(memory_space=pltpu.VMEM)
SM=pl.BlockSpec(memory_space=pltpu.SMEM)
def shape(s,t=f32): return jax.ShapeDtypeStruct(s,t)

def run_forward(lengths,qp,gp,near,far,qr,gr,kvr,KC=512):
    span=qr.shape[0]; half=near.shape[0]; share=qp.shape[0]; n=span+share
    return pl.pallas_call(functools.partial(forward,KC),
        out_shape=(shape(qp.shape,bf16),shape(qr.shape,bf16),shape((D+16,n)),shape((LINES,2,span//HEADS+TILE,2*D)),shape((half,n)),shape((half,n))),
        in_specs=[SM]+[V]*7,out_specs=(V,)*6,
        scratch_shapes=[pltpu.VMEM((span,span),f32)],
        cost_estimate=pl.CostEstimate(flops=5*n*half*2*D,bytes_accessed=2**23,transcendentals=4*n*half),
        compiler_params=pltpu.CompilerParams(vmem_limit_bytes=22*1024*1024),name="forward")(lengths,qp,gp,near,far,qr,gr,kvr)

def run_backward(last,qp,gp,kv,qr,gr,e,carry,KC=512):
    n=carry.shape[1]; half=kv.shape[0]
    return pl.pallas_call(functools.partial(backward,KC,last),
        out_shape=((shape(qr.shape,bf16),shape(qp.shape,bf16)) if last else (shape(carry.shape),))+(shape(kv.shape),),
        in_specs=[V]*7,out_specs=(V,)*(2+last),
        cost_estimate=pl.CostEstimate(flops=50*n*half*2*D,bytes_accessed=2**22,transcendentals=n*half),
        compiler_params=pltpu.CompilerParams(vmem_limit_bytes=28*1024*1024),name="backward")(qp,gp,kv,qr,gr,e,carry)

def run_combine(mine,other):
    n=mine.shape[0]//CORE_CHIPS
    return pl.pallas_call(combine,out_shape=shape((CORE_CHIPS,n+TILE,2*D)),in_specs=[V]*2,out_specs=V,
        compiler_params=pltpu.CompilerParams(vmem_limit_bytes=16*1024*1024),name="combine")(mine,other)

def swap(x): return lax.ppermute(x,"core",[(0,1),(1,0)])
def spread(x,axes): return lax.all_to_all(x,axes,0,0,tiled=True)
def copies(x,n): return jnp.broadcast_to(x[None],(n,)+x.shape)

def unpack(x):
    rest=jnp.exp2(x[:,-TILE:].astype(f32))
    x=x[:,:-TILE].astype(f32).reshape(x.shape[0],-1,TILE,x.shape[2])
    return x*rest[:,None]

def turn(x,by): return lax.ppermute(x,"y",[(i,(i+by)%LINES) for i in range(LINES)])

def on_device(qp,kvp,qr,kvr,gp,gr,lengths):
    head=lax.axis_index(HEAD)
    piece=lax.dynamic_slice_in_dim(kvp,head*ROWS,ROWS,0)
    line=spread(copies(piece,LONG),"z").reshape(-1,2*D)
    near=spread(copies(line,CORE_CHIPS),PLANE).reshape(-1,2*D)
    far=swap(near)
    op,our,carry,own,enear,efar=run_forward(lengths,qp,gp,near,far,qr,gr,kvr)
    turns=[turn(own[i].astype(jnp.float16),i) for i in range(1,LINES)]
    carry,dfar=run_backward(False,qp,gp,far,qr,gr,efar,carry)
    recv=swap(dfar)
    carry,turns=lax.optimization_barrier((carry,turns))
    own=sum([unpack(x) for x in turns],unpack(own[0])).reshape(2,-1,2*D)
    met=lax.ppermute(own[1],"x_lo",[(0,1),(1,0)])
    dqr,dqp,dnear=run_backward(True,qp,gp,near,qr,gr,enear,carry)
    chip=run_combine(dnear,recv)
    chip,met=lax.optimization_barrier((chip,met))
    chip,own=lax.optimization_barrier((chip.astype(jnp.float16),own[0]+met))
    line=unpack(spread(chip,PLANE)).sum(0)
    strip=spread(line.reshape(LONG,ROWS,2*D),"z").sum(0)
    done=jnp.concatenate([strip,own]).astype(bf16)
    done=spread(copies(done,HEADS),HEAD)
    mine=done[:,ROWS:].reshape(LINES,2,-1,2*D).transpose(1,0,2,3).reshape(-1,2*D)
    return (op,our,dqp,dqr,done[:,:ROWS].reshape(-1,2*D),mine)

def solution(mesh):
    P=jax.sharding.PartitionSpec
    fine=jax.sharding.Mesh(mesh.devices.reshape(2,LONG,2,4,2),SEQ+HEAD)
    rows_,cache=P(SEQ,HEAD),P(SEQ,None)
    return jax.shard_map(on_device,mesh=fine,
        in_specs=(rows_,cache,rows_,cache,rows_,rows_,P(SEQ)),
        out_specs=(rows_,rows_,rows_,rows_,cache,cache),check_vma=False)
```

time: 123 us -> 120 us (0.976)
  Pallas kernels: 25.4 us -> 23 us
  waiting for transfers between devices: 4.01 us -> 5.41 us
    ppermute x3, waiting for transfers between devices: 0.01 us -> 3.4 us  [turn(): return lax.ppermute(x, 'y', [(i, (i + by) % LINES) for i in range(LINES)])]
    pallas_call x2, Pallas kernels: 13.7 us -> 10.8 us  [run_backward(): pl.pallas_call(functools.partial(backward, KC, last), out_shape=((shape(q...]
    ppermute x1, waiting for transfers between devices: 1.31 us -> 0.01 us  [on_device(): met = lax.ppermute(own[1], 'x_lo', [(0, 1), (1, 0)])]
  transfers between devices with their start and end apart: 6 -> 6, of which waited for: 3 -> 3; matrix products, arithmetic and copies ran while one was open for 0% -> 0% of each run, Pallas kernels for 11% -> 9%
where the time goes in v5:
time: 120 us; the launch traced here: 119 us
  blocking collectives  82.6 us (69%)
  Pallas kernels  23 us (19%)
  waiting for transfers between devices  5.41 us (5%)
  starting transfers between devices  3.71 us (3%)
  local copies, waits for them, and re-layouts  2.56 us (2%)
  between operations  1.5 us (1%)
    all_to_all x5, blocking collectives, spread(): return lax.all_to_all(x, axes, 0, 0, tiled=True)  82.6 us
    pallas_call x1, Pallas kernels, run_forward(): pl.pallas_call(functools.partial(forward, KC), out_shape=(shape(qp.shape,...  11.9 us
    pallas_call x2, Pallas kernels, run_backward(): pl.pallas_call(functools.partial(backward, KC, last), out_shape=((shape(q...  10.8 us
    ppermute x3, waiting for transfers between devices, turn(): return lax.ppermute(x, 'y', [(i, (i + by) % LINES) for i in range(LINES)])  3.4 us
  transfers between devices with their start and end apart: 6, of which 3 were waited for; matrix products, arithmetic and copies ran while one was open for 0% of the time, Pallas kernels for 9%

profile of v5, /device:TPU:2, one launch (start us, length us, event | category | flops | bytes accessed | tf_op | source)
XLA Modules:
  0.0 119.5 jit_solution(5526889563746234394)
XLA Ops:
  0.6 0.0 copy-start
  0.7 0.8 copy-done
  1.5 16.6 %all_to_all.25 = bf16[8,16,256]{2,1,0:T(8,128)(2,1)S(1)} all-to-all(bf16[8,16,256]{2,1,0:T(8,128)(2,1)S(1)} %broadcast_in_dim.8), channel_id=1, replica_groups=mesh['x_hi'=2,'z'=8,'core'=2,'y'=4,'x_lo'=2] {'z'}, dimensions={0} | all-to-all | bytes 131072 | tf_op jit(solution)/shard_map/all_to_all | solution.py:185
  18.1 0.1 broadcast_in_dim.10
  18.2 22.2 %all_to_all.26 = bf16[16,128,256]{2,1,0:T(8,128)(2,1)S(1)} all-to-all(bf16[16,128,256]{2,1,0:T(8,128)(2,1)S(1)} %broadcast_in_dim.10), channel_id=1, replica_groups=mesh['x_hi'=2,'z'=8,'core'=2,'y'=4,'x_lo'=2] {'x_hi','y','x_lo'}, dimensions={0} | all-to-all | bytes 2097152 | tf_op jit(solution)/shard_map/all_to_all | solution.py:185
  40.4 0.0 collective-permute-start
  41.1 2.0 %collective-permute-done.far.kv = bf16[2048,256]{1,0:T(8,128)(2,1)S(1)} collective-permute-done((bf16[2048,256]{1,0:T(8,128)(2,1)S(1)}, bf16[2048,256]{1,0:T(8,128)(2,1)S(1)}, u32[]{:S(2)}, u32[]{:S(2)}) %collective-permute-start) | collective-permute-done | bytes 1048608 | tf_op jit(solution)/shard_map/ppermute | solution.py:184
  43.1 0.0 copy-done.5
  43.1 11.9 %forward.1 = (bf16[128,128]{1,0:T(8,128)(2,1)}, bf16[1024,128]{1,0:T(8,128)(2,1)}, f32[144,1152]{1,0:T(8,128)S(1)}, f32[4,2,136,256]{3,2,1,0:T(8,128)S(1)}, f32[...) custom-call(s32[1]{0:T(128)S(6)} %copy.15.info, bf16[128,128]{1,0:T(8,128)(2,1)S(1)} %copy-done.4, ...), custom_call_target="tpu_custom_call" | custom-call | flops 3019898880 | bytes 8388608 | tf_op jit(solution)/shard_map/forward/pallas_call | solution.py:164
  55.0 0.1 convert.14
  55.1 0.1 slice_bitcast_fusion.2
  55.2 0.7 collective-permute-start.3
  55.9 0.3 collective-permute-start.2
  56.2 1.1 collective-permute-start.1
  57.3 5.0 %backward.2 = (f32[144,1152]{1,0:T(8,128)S(1)}, f32[2048,256]{1,0:T(8,128)S(1)}) custom-call(bf16[128,128]{1,0:T(8,128)(2,1)S(1)} %copy-done.4, bf16[128,128]{1,0:T(8,128)(2,1)S(1)} %copy-done.5, bf16[2048,256]{1,0:T(8,128)(2,1)S(1)} %collective-permute-done.far.kv, bf16[1024,128]{1,0:T(8,128)(2,1)S(1)} %copy-done.2, bf16[1024,128]{1,0:T(8,128)(2,1)S(1)} %copy-done.3, ...), custom_call_target="tpu_custom_call" | custom-call | flops 30198988800 | bytes 4194304 | tf_op jit(solution)/shard_map/backward/pallas_call | solution.py:173
  62.3 0.1 collective-permute-start.4
  62.4 0.0 collective-permute-done.3
  62.4 1.5 %collective-permute-done.2 = f16[2,136,256]{2,1,0:T(8,128)(2,1)S(1)} collective-permute-done((f16[2,136,256]{2,1,0:T(8,128)(2,1)S(1)}, f16[2,136,256]{2,1,0:T(8,128)(2,1)S(1)}, u32[]{:S(2)}, u32[]{:S(2)}) %collective-permute-start.2) | collective-permute-done | bytes 139296 | tf_op jit(solution)/shard_map/ppermute | solution.py:193
  63.9 1.9 %collective-permute-done.1 = f16[2,136,256]{2,1,0:T(8,128)(2,1)S(1)} collective-permute-done((f16[2,136,256]{2,1,0:T(8,128)(2,1)S(1)}, f16[2,136,256]{2,1,0:T(8,128)(2,1)S(1)}, u32[]{:S(2)}, u32[]{:S(2)}) %collective-permute-start.1) | collective-permute-done | bytes 139296 | tf_op jit(solution)/shard_map/ppermute | solution.py:193
  65.8 0.1 fusion.4
  65.9 1.5 %collective-permute-start.5 = (f32[128,256]{1,0:T(8,128)S(1)}, f32[128,256]{1,0:T(8,128)S(1)}, u32[]{:S(2)}, u32[]{:S(2)}) collective-permute-start(f32[128,256]{1,0:T(8,128)S(1)} %slice_bitcast_fusion.6), channel_id=1, source_target_pairs={{0,1},{1,0},{2,3},{3,2},{4,5},{5,4},{6,7},{7,6},{8,9},{9,8},{10,11... | collective-permute-start | bytes 393224 | tf_op jit(solution)/shard_map/ppermute | solution.py:207
  67.5 5.8 %backward.3 = (bf16[1024,128]{1,0:T(8,128)(2,1)}, bf16[128,128]{1,0:T(8,128)(2,1)}, f32[2048,256]{1,0:T(8,128)S(1)}) custom-call(bf16[128,128]{1,0:T(8,128)(2,1)S(1)} %copy-done.4, bf16[128,128]{1,0:T(8,128)(2,1)S(1)} %copy-done.5, bf16[2048,256]{1,0:T(8,128)(2,1)S(1)} %bitcast.47, bf16[1024,128]{1,0:T(8,128)(2,1)S(1)} %copy-done.2, ...), custom_call_target="tpu_custom_call" | custom-call | flops 30198988800 | bytes 4194304 | tf_op jit(solution)/shard_map/backward/pallas_call | solution.py:173
  73.2 0.0 collective-permute-done.4.other
  73.2 0.3 combine.1
  73.6 0.0 collective-permute-done.5
  73.6 0.2 convert_element_type.44
  73.8 20.7 %all_to_all.27 = f16[16,136,256]{2,1,0:T(8,128)(2,1)S(1)} all-to-all(f16[16,136,256]{2,1,0:T(8,128)(2,1)S(1)} %convert_element_type.44), channel_id=1, replica_groups=mesh['x_hi'=2,'z'=8,'core'=2,'y'=4,'x_lo'=2] {'x_hi','y','x_lo'}, dimensions={0} | all-to-all | bytes 2228224 | tf_op jit(solution)/shard_map/all_to_all | solution.py:185
  94.5 0.2 fusion
  94.7 11.5 %all_to_all.28 = f32[8,16,256]{2,1,0:T(8,128)S(1)} all-to-all(f32[8,16,256]{2,1,0:T(8,128)S(1)} %bitcast.49), channel_id=1, replica_groups=mesh['x_hi'=2,'z'=8,'core'=2,'y'=4,'x_lo'=2] {'z'}, dimensions={0} | all-to-all | bytes 262144 | tf_op jit(solution)/shard_map/all_to_all | solution.py:185
  106.3 11.7 %all_to_all.29 = bf16[8,144,256]{2,1,0:T(8,128)(2,1)S(1)} all-to-all(bf16[8,144,256]{2,1,0:T(8,128)(2,1)S(1)} %broadcast_in_dim.11), channel_id=1, replica_groups=mesh['x_hi'=2,'z'=8,'core'=2,'y'=4,'x_lo'=2] {'y','x_lo'}, dimensions={0} | all-to-all | bytes 1179648 | tf_op jit(solution)/shard_map/all_to_all | solution.py:185
  118.0 0.8 copy.14
  118.9 0.6 slice.86
  (22 shorter events, 0.2 us)
Async XLA Ops:
  0.6 0.8 copy-start
  0.6 42.4 %copy-start.3 = (bf16[1024,128]{1,0:T(8,128)(2,1)S(1)}, bf16[1024,128]{1,0:T(8,128)(2,1)}, u32[]{:S(2)}) copy-start(bf16[1024,128]{1,0:T(8,128)(2,1)} %gr.5) | copy-start | bytes 786436
  0.7 42.4 %copy-start.5 = (bf16[128,128]{1,0:T(8,128)(2,1)S(1)}, bf16[128,128]{1,0:T(8,128)(2,1)}, u32[]{:S(2)}) copy-start(bf16[128,128]{1,0:T(8,128)(2,1)} %gp.5) | copy-start | bytes 98308
  0.7 42.4 %copy-start.2 = (bf16[1024,128]{1,0:T(8,128)(2,1)S(1)}, bf16[1024,128]{1,0:T(8,128)(2,1)}, u32[]{:S(2)}) copy-start(bf16[1024,128]{1,0:T(8,128)(2,1)} %qr.5) | copy-start | bytes 786436
  0.7 42.4 %copy-start.4 = (bf16[128,128]{1,0:T(8,128)(2,1)S(1)}, bf16[128,128]{1,0:T(8,128)(2,1)}, u32[]{:S(2)}) copy-start(bf16[128,128]{1,0:T(8,128)(2,1)} %qp.5) | copy-start | bytes 98308
  0.7 42.4 %copy-start.1 = (bf16[1024,256]{1,0:T(8,128)(2,1)S(1)}, bf16[1024,256]{1,0:T(8,128)(2,1)}, u32[]{:S(2)}) copy-start(bf16[1024,256]{1,0:T(8,128)(2,1)} %kvr.1) | copy-start | bytes 1572868
  40.4 2.7 %collective-permute-start = (bf16[2048,256]{1,0:T(8,128)(2,1)S(1)}, bf16[2048,256]{1,0:T(8,128)(2,1)S(1)}, u32[]{:S(2)}, u32[]{:S(2)}) collective-permute-start(bf16[2048,256]{1,0:T(8,128)(2,1)S(1)} %bitcast.45), channel_id=1, source_target_pairs={{0,8},{8,0},{1,9},{9,1},{2,10},{10,2},{3,11},{11,3},{4,12},{12,4},... | collective-permute-start | bytes 3145736 | tf_op jit(solution)/shard_map/ppermute | solution.py:184
  55.2 7.2 %collective-permute-start.3 = (f16[2,136,256]{2,1,0:T(8,128)(2,1)S(1)}, f16[2,136,256]{2,1,0:T(8,128)(2,1)S(1)}, u32[]{:S(2)}, u32[]{:S(2)}) collective-permute-start(f16[2,136,256]{2,1,0:T(8,128)(2,1)S(1)} %get-tuple-element.44), channel_id=1, source_target_pairs={{0,6},{2,0},{4,2},{6,4},{1,7},{3,1},{5,3},{7,5},{8,14},{10,8},{12,... | collective-permute-start | bytes 417800 | tf_op jit(solution)/shard_map/ppermute | solution.py:193
  55.9 8.1 %collective-permute-start.2 = (f16[2,136,256]{2,1,0:T(8,128)(2,1)S(1)}, f16[2,136,256]{2,1,0:T(8,128)(2,1)S(1)}, u32[]{:S(2)}, u32[]{:S(2)}) collective-permute-start(f16[2,136,256]{2,1,0:T(8,128)(2,1)S(1)} %get-tuple-element.45), channel_id=1, source_target_pairs={{0,4},{2,6},{4,0},{6,2},{1,5},{3,7},{5,1},{7,3},{8,12},{10,14},{12... | collective-permute-start | bytes 417800 | tf_op jit(solution)/shard_map/ppermute | solution.py:193
  56.2 9.6 %collective-permute-start.1 = (f16[2,136,256]{2,1,0:T(8,128)(2,1)S(1)}, f16[2,136,256]{2,1,0:T(8,128)(2,1)S(1)}, u32[]{:S(2)}, u32[]{:S(2)}) collective-permute-start(f16[2,136,256]{2,1,0:T(8,128)(2,1)S(1)} %get-tuple-element.46), channel_id=1, source_target_pairs={{0,2},{2,4},{4,6},{6,0},{1,3},{3,5},{5,7},{7,1},{8,10},{10,12},{12... | collective-permute-start | bytes 417800 | tf_op jit(solution)/shard_map/ppermute | solution.py:193
  62.3 11.0 %collective-permute-start.4 = (f32[2048,256]{1,0:T(8,128)S(1)}, f32[2048,256]{1,0:T(8,128)S(1)}, u32[]{:S(2)}, u32[]{:S(2)}) collective-permute-start(f32[2048,256]{1,0:T(8,128)S(1)} %get-tuple-element.36), channel_id=1, source_target_pairs={{0,8},{8,0},{1,9},{9,1},{2,10},{10,2},{3,11},{11,3},{4,12},{12,4},... | collective-permute-start | bytes 6291464 | tf_op jit(solution)/shard_map/ppermute | solution.py:184
  65.9 7.7 %collective-permute-start.5 = (f32[128,256]{1,0:T(8,128)S(1)}, f32[128,256]{1,0:T(8,128)S(1)}, u32[]{:S(2)}, u32[]{:S(2)}) collective-permute-start(f32[128,256]{1,0:T(8,128)S(1)} %slice_bitcast_fusion.6), channel_id=1, source_target_pairs={{0,1},{1,0},{2,3},{3,2},{4,5},{5,4},{6,7},{7,6},{8,9},{9,8},{10,11... | collective-permute-start | bytes 393224 | tf_op jit(solution)/shard_map/ppermute | solution.py:207

commit v6 on v5

--- a/solution.py
+++ b/solution.py
@@ -9,6 +9,7 @@
 RATE=math.log2(math.e)*SCALE
 FAR=1e30
 OWN=256
+EARLY=512
 SEQ=("x_hi","z","core")
 HEAD=("y","x_lo")
 PLANE=("x_hi","y","x_lo")
@@ -20,7 +21,7 @@
 ROWS=16
 
 def dot(a,b): return jnp.dot(a,b,preferred_element_type=f32)
-def flip(x): return x.astype(f32).T.astype(bf16)
+def flip(x): return x.T
 def fold(x): return x.reshape(x.shape[0]//8,8,x.shape[1])
 def rows(i,n): return pl.ds(i*n,n)
 def loop(n,step,init):
@@ -123,30 +124,33 @@
         dq=y if j==0 else jnp.concatenate([dq[:,:j*OWN],y],axis=1)
     carry[:D,:]=jnp.concatenate([dq,jnp.zeros((D,share),f32)],axis=1)
 
-def combine(mine,other,out):
-    n=mine.shape[0]//CORE_CHIPS
+def combine(first,rest,other,out):
+    n=other.shape[0]//CORE_CHIPS
     for b in range(CORE_CHIPS):
-        x=mine[rows(b,n),:]+other[rows(b,n),:]
-        pack(out,(b,),slice(0,2*D),x)
-
-def backward(KC,last,qp,gp,kv,qr,gr,e,carry,*out):
-    *out,grad=out
-    half=kv.shape[0]; span=qr.shape[0]; share=qp.shape[0]
+        mine=first[rows(b,n),:] if b*n<EARLY else rest[pl.ds(b*n-EARLY,n),:]
+        pack(out,(b,),slice(0,2*D),mine+other[rows(b,n),:])
+
+def backward(KC,last,qp,gp,qr,gr,carry,near,enear,*out):
+    half=near.shape[0]; span=qr.shape[0]; share=qp.shape[0]
+    if last:
+        *out,gnear=out
+        work=[(near,enear,gnear,i,i-EARLY//KC) for i in range(EARLY//KC,half//KC)]
+    else:
+        far,efar,*out,gnear,gfar=out
+        work=[(far,efar,gfar,i,i) for i in range(half//KC)]+[(near,enear,gnear,i,i) for i in range(EARLY//KC)]
     gt=jnp.concatenate([flip(gr[...]),flip(gp[...])],axis=1)
     q=jnp.concatenate([qr[...],qp[...]],axis=0)
     g=jnp.concatenate([gr[...],gp[...]],axis=0)
     inv=carry[D:D+1,:]; delta=carry[D+8:D+9,:]
-    def step(i,dq):
+    dq=carry[:D,:]
+    for kv,e,grad,i,o in work:
         a=rows(i,KC)
         dp=dot(kv[a,D:],gt)
         p=e[a,:]*inv
         ds=(p*(dp-delta)).astype(bf16)
-        dv=dot(p.astype(bf16),g)
-        dk=dot(ds,q)*SCALE
-        grad[a,D:]=dv
-        grad[a,:D]=dk
-        return dq+dot(flip(kv[a,:D]),ds)
-    dq=loop(half//KC,step,carry[:D,:])
+        grad[rows(o,KC),D:]=dot(p.astype(bf16),g)
+        grad[rows(o,KC),:D]=dot(ds,q)*SCALE
+        dq=dq+dot(flip(kv[a,:D]),ds)
     if not last:
         out[0][:D,:]=dq
         out[0][D:,:]=carry[D:,:]
@@ -168,18 +172,21 @@
         cost_estimate=pl.CostEstimate(flops=5*n*half*2*D,bytes_accessed=2**23,transcendentals=4*n*half),
         compiler_params=pltpu.CompilerParams(vmem_limit_bytes=22*1024*1024),name="forward")(lengths,qp,gp,near,far,qr,gr,kvr)
 
-def run_backward(last,qp,gp,kv,qr,gr,e,carry,KC=512):
-    n=carry.shape[1]; half=kv.shape[0]
+def run_backward(last,qp,gp,qr,gr,carry,near,enear,*far,KC=512):
+    n=carry.shape[1]; half=near.shape[0]
+    if last:
+        out=(shape(qr.shape,bf16),shape(qp.shape,bf16),shape((half-EARLY,2*D)))
+    else:
+        out=(shape(carry.shape),shape((EARLY,2*D)),shape(near.shape))
     return pl.pallas_call(functools.partial(backward,KC,last),
-        out_shape=((shape(qr.shape,bf16),shape(qp.shape,bf16)) if last else (shape(carry.shape),))+(shape(kv.shape),),
-        in_specs=[V]*7,out_specs=(V,)*(2+last),
+        out_shape=out,in_specs=[V]*(7+len(far)),out_specs=(V,)*3,
         cost_estimate=pl.CostEstimate(flops=50*n*half*2*D,bytes_accessed=2**22,transcendentals=n*half),
-        compiler_params=pltpu.CompilerParams(vmem_limit_bytes=28*1024*1024),name="backward")(qp,gp,kv,qr,gr,e,carry)
-
-def run_combine(mine,other):
-    n=mine.shape[0]//CORE_CHIPS
-    return pl.pallas_call(combine,out_shape=shape((CORE_CHIPS,n+TILE,2*D)),in_specs=[V]*2,out_specs=V,
-        compiler_params=pltpu.CompilerParams(vmem_limit_bytes=16*1024*1024),name="combine")(mine,other)
+        compiler_params=pltpu.CompilerParams(vmem_limit_bytes=20*1024*1024),name="backward")(qp,gp,qr,gr,carry,near,enear,*far)
+
+def run_combine(first,rest,other):
+    n=other.shape[0]//CORE_CHIPS
+    return pl.pallas_call(combine,out_shape=shape((CORE_CHIPS,n+TILE,2*D)),in_specs=[V]*3,out_specs=V,
+        compiler_params=pltpu.CompilerParams(vmem_limit_bytes=16*1024*1024),name="combine")(first,rest,other)
 
 def swap(x): return lax.ppermute(x,"core",[(0,1),(1,0)])
 def spread(x,axes): return lax.all_to_all(x,axes,0,0,tiled=True)
@@ -200,13 +207,13 @@
     far=swap(near)
     op,our,carry,own,enear,efar=run_forward(lengths,qp,gp,near,far,qr,gr,kvr)
     turns=[turn(own[i].astype(jnp.float16),i) for i in range(1,LINES)]
-    carry,dfar=run_backward(False,qp,gp,far,qr,gr,efar,carry)
+    carry,dearly,dfar=run_backward(False,qp,gp,qr,gr,carry,near,enear,far,efar)
     recv=swap(dfar)
     carry,turns=lax.optimization_barrier((carry,turns))
     own=sum([unpack(x) for x in turns],unpack(own[0])).reshape(2,-1,2*D)
     met=lax.ppermute(own[1],"x_lo",[(0,1),(1,0)])
-    dqr,dqp,dnear=run_backward(True,qp,gp,near,qr,gr,enear,carry)
-    chip=run_combine(dnear,recv)
+    dqr,dqp,dnear=run_backward(True,qp,gp,qr,gr,carry,near,enear)
+    chip=run_combine(dearly,dnear,recv)
     chip,met=lax.optimization_barrier((chip,met))
     chip,own=lax.optimization_barrier((chip.astype(jnp.float16),own[0]+met))
     line=unpack(spread(chip,PLANE)).sum(0)

time: 120 us -> 119 us (level)
  waiting for transfers between devices: 5.41 us -> 4.2 us
  blocking collectives: 82.6 us -> 83.8 us
    ppermute x3, waiting for transfers between devices: 3.4 us -> 2.19 us  [turn(): return lax.ppermute(x, 'y', [(i, (i + by) % LINES) for i in range(LINES)])]
where the time goes in v6:
time: 119 us
  blocking collectives  83.8 us (70%)
  Pallas kernels  21.9 us (18%)
  waiting for transfers between devices  4.2 us (4%)
  starting transfers between devices  4.12 us (3%)
  local copies, waits for them, and re-layouts  2.56 us (2%)
  between operations  1.49 us (1%)
    all_to_all x5, blocking collectives, spread(): return lax.all_to_all(x, axes, 0, 0, tiled=True)  83.8 us
    pallas_call x1, Pallas kernels, run_forward(): pl.pallas_call(functools.partial(forward, KC), out_shape=(shape(qp.shape,...  10.8 us
    pallas_call x2, Pallas kernels, run_backward(): pl.pallas_call(functools.partial(backward, KC, last), out_shape=out, in_s...  10.8 us
  transfers between devices with their start and end apart: 6, of which 3 were waited for; matrix products, arithmetic and copies ran while one was open for 0% of the time, Pallas kernels for 9%

profile of v6, /device:TPU:2, one launch (start us, length us, event | category | flops | bytes accessed | tf_op | source)
XLA Modules:
  0.0 118.9 jit_solution(6346240695106285692)
XLA Ops:
  0.6 0.0 copy-start
  0.7 0.8 copy-done
  1.5 16.6 %all_to_all.25 = bf16[8,16,256]{2,1,0:T(8,128)(2,1)S(1)} all-to-all(bf16[8,16,256]{2,1,0:T(8,128)(2,1)S(1)} %broadcast_in_dim.8), channel_id=1, replica_groups=mesh['x_hi'=2,'z'=8,'core'=2,'y'=4,'x_lo'=2] {'z'}, dimensions={0} | all-to-all | bytes 131072 | tf_op jit(solution)/shard_map/all_to_all | solution.py:192
  18.1 0.1 broadcast_in_dim.10
  18.2 22.2 %all_to_all.26 = bf16[16,128,256]{2,1,0:T(8,128)(2,1)S(1)} all-to-all(bf16[16,128,256]{2,1,0:T(8,128)(2,1)S(1)} %broadcast_in_dim.10), channel_id=1, replica_groups=mesh['x_hi'=2,'z'=8,'core'=2,'y'=4,'x_lo'=2] {'x_hi','y','x_lo'}, dimensions={0} | all-to-all | bytes 2097152 | tf_op jit(solution)/shard_map/all_to_all | solution.py:192
  40.4 0.0 collective-permute-start
  41.1 2.0 %collective-permute-done.far.out_0_ = bf16[2048,256]{1,0:T(8,128)(2,1)S(1)} collective-permute-done((bf16[2048,256]{1,0:T(8,128)(2,1)S(1)}, bf16[2048,256]{1,0:T(8,128)(2,1)S(1)}, u32[]{:S(2)}, u32[]{:S(2)}) %collective-permute-start) | collective-permute-done | bytes 1048608 | tf_op jit(solution)/shard_map/ppermute | solution.py:191
  43.1 0.0 copy-done.5
  43.1 10.8 %forward.1 = (bf16[128,128]{1,0:T(8,128)(2,1)}, bf16[1024,128]{1,0:T(8,128)(2,1)}, f32[144,1152]{1,0:T(8,128)S(1)}, f32[4,2,136,256]{3,2,1,0:T(8,128)S(1)}, f32[...) custom-call(s32[1]{0:T(128)S(6)} %copy.15.info, bf16[128,128]{1,0:T(8,128)(2,1)S(1)} %copy-done.4, ...), custom_call_target="tpu_custom_call" | custom-call | flops 3019898880 | bytes 8388608 | tf_op jit(solution)/shard_map/forward/pallas_call | solution.py:168
  53.9 0.1 convert.14
  54.0 0.1 slice_bitcast_fusion.2
  54.1 0.9 collective-permute-start.3
  55.0 0.3 collective-permute-start.2
  55.4 1.1 collective-permute-start.1
  56.4 6.2 %backward.2 = (f32[144,1152]{1,0:T(8,128)S(1)}, f32[512,256]{1,0:T(8,128)S(1)}, f32[2048,256]{1,0:T(8,128)S(1)}) custom-call(bf16[128,128]{1,0:T(8,128)(2,1)S(1)} %copy-done.4, bf16[128,128]{1,0:T(8,128)(2,1)S(1)} %copy-done.5, bf16[1024,128]{1,0:T(8,128)(2,1)S(1)} %copy-done.2, bf16[1024,128]{1,0:T(8,128)(2,1)S(1)} %copy-done.3, ...), custom_call_target="tpu_custom_call" | custom-call | flops 30198988800 | bytes 4194304 | tf_op jit(solution)/shard_map/backward/pallas_call | solution.py:181
  62.6 0.1 collective-permute-start.4
  62.7 0.0 collective-permute-done.3
  62.7 0.3 collective-permute-done.2
  63.1 1.9 %collective-permute-done.1 = f16[2,136,256]{2,1,0:T(8,128)(2,1)S(1)} collective-permute-done((f16[2,136,256]{2,1,0:T(8,128)(2,1)S(1)}, f16[2,136,256]{2,1,0:T(8,128)(2,1)S(1)}, u32[]{:S(2)}, u32[]{:S(2)}) %collective-permute-start.1) | collective-permute-done | bytes 139296 | tf_op jit(solution)/shard_map/ppermute | solution.py:200
  65.0 0.1 fusion.4
  65.1 1.7 %collective-permute-start.5 = (f32[128,256]{1,0:T(8,128)S(1)}, f32[128,256]{1,0:T(8,128)S(1)}, u32[]{:S(2)}, u32[]{:S(2)}) collective-permute-start(f32[128,256]{1,0:T(8,128)S(1)} %slice_bitcast_fusion.6), channel_id=1, source_target_pairs={{0,1},{1,0},{2,3},{3,2},{4,5},{5,4},{6,7},{7,6},{8,9},{9,8},{10,11... | collective-permute-start | bytes 393224 | tf_op jit(solution)/shard_map/ppermute | solution.py:214
  66.8 4.6 %backward.3 = (bf16[1024,128]{1,0:T(8,128)(2,1)}, bf16[128,128]{1,0:T(8,128)(2,1)}, f32[1536,256]{1,0:T(8,128)S(1)}) custom-call(bf16[128,128]{1,0:T(8,128)(2,1)S(1)} %copy-done.4, bf16[128,128]{1,0:T(8,128)(2,1)S(1)} %copy-done.5, bf16[1024,128]{1,0:T(8,128)(2,1)S(1)} %copy-done.2, bf16[1024,128]{1,0:T(8,128)(2,1)S(1)} %copy-done.3, ...), custom_call_target="tpu_custom_call" | custom-call | flops 30198988800 | bytes 4194304 | tf_op jit(solution)/shard_map/backward/pallas_call | solution.py:181
  71.4 0.0 collective-permute-done.4.other
  71.4 0.4 combine.1
  71.8 0.0 collective-permute-done.5
  71.8 0.2 convert_element_type.44
  72.0 21.8 %all_to_all.27 = f16[16,136,256]{2,1,0:T(8,128)(2,1)S(1)} all-to-all(f16[16,136,256]{2,1,0:T(8,128)(2,1)S(1)} %convert_element_type.44), channel_id=1, replica_groups=mesh['x_hi'=2,'z'=8,'core'=2,'y'=4,'x_lo'=2] {'x_hi','y','x_lo'}, dimensions={0} | all-to-all | bytes 2228224 | tf_op jit(solution)/shard_map/all_to_all | solution.py:192
  93.9 0.2 fusion
  94.1 11.5 %all_to_all.28 = f32[8,16,256]{2,1,0:T(8,128)S(1)} all-to-all(f32[8,16,256]{2,1,0:T(8,128)S(1)} %bitcast.50), channel_id=1, replica_groups=mesh['x_hi'=2,'z'=8,'core'=2,'y'=4,'x_lo'=2] {'z'}, dimensions={0} | all-to-all | bytes 262144 | tf_op jit(solution)/shard_map/all_to_all | solution.py:192
  105.6 11.7 %all_to_all.29 = bf16[8,144,256]{2,1,0:T(8,128)(2,1)S(1)} all-to-all(bf16[8,144,256]{2,1,0:T(8,128)(2,1)S(1)} %broadcast_in_dim.11), channel_id=1, replica_groups=mesh['x_hi'=2,'z'=8,'core'=2,'y'=4,'x_lo'=2] {'y','x_lo'}, dimensions={0} | all-to-all | bytes 1179648 | tf_op jit(solution)/shard_map/all_to_all | solution.py:192
  117.4 0.8 copy.14
  118.2 0.6 slice.86
  (22 shorter events, 0.2 us)
Async XLA Ops:
  0.6 0.8 copy-start
  0.6 42.4 %copy-start.3 = (bf16[1024,128]{1,0:T(8,128)(2,1)S(1)}, bf16[1024,128]{1,0:T(8,128)(2,1)}, u32[]{:S(2)}) copy-start(bf16[1024,128]{1,0:T(8,128)(2,1)} %gr.5) | copy-start | bytes 786436
  0.7 42.4 %copy-start.5 = (bf16[128,128]{1,0:T(8,128)(2,1)S(1)}, bf16[128,128]{1,0:T(8,128)(2,1)}, u32[]{:S(2)}) copy-start(bf16[128,128]{1,0:T(8,128)(2,1)} %gp.5) | copy-start | bytes 98308
  0.7 42.4 %copy-start.2 = (bf16[1024,128]{1,0:T(8,128)(2,1)S(1)}, bf16[1024,128]{1,0:T(8,128)(2,1)}, u32[]{:S(2)}) copy-start(bf16[1024,128]{1,0:T(8,128)(2,1)} %qr.5) | copy-start | bytes 786436
  0.7 42.4 %copy-start.4 = (bf16[128,128]{1,0:T(8,128)(2,1)S(1)}, bf16[128,128]{1,0:T(8,128)(2,1)}, u32[]{:S(2)}) copy-start(bf16[128,128]{1,0:T(8,128)(2,1)} %qp.5) | copy-start | bytes 98308
  0.7 42.4 %copy-start.1 = (bf16[1024,256]{1,0:T(8,128)(2,1)S(1)}, bf16[1024,256]{1,0:T(8,128)(2,1)}, u32[]{:S(2)}) copy-start(bf16[1024,256]{1,0:T(8,128)(2,1)} %kvr.1) | copy-start | bytes 1572868
  40.4 2.7 %collective-permute-start = (bf16[2048,256]{1,0:T(8,128)(2,1)S(1)}, bf16[2048,256]{1,0:T(8,128)(2,1)S(1)}, u32[]{:S(2)}, u32[]{:S(2)}) collective-permute-start(bf16[2048,256]{1,0:T(8,128)(2,1)S(1)} %bitcast.45), channel_id=1, source_target_pairs={{0,8},{8,0},{1,9},{9,1},{2,10},{10,2},{3,11},{11,3},{4,12},{12,4},... | collective-permute-start | bytes 3145736 | tf_op jit(solution)/shard_map/ppermute | solution.py:191
  54.1 8.6 %collective-permute-start.3 = (f16[2,136,256]{2,1,0:T(8,128)(2,1)S(1)}, f16[2,136,256]{2,1,0:T(8,128)(2,1)S(1)}, u32[]{:S(2)}, u32[]{:S(2)}) collective-permute-start(f16[2,136,256]{2,1,0:T(8,128)(2,1)S(1)} %get-tuple-element.46), channel_id=1, source_target_pairs={{0,6},{2,0},{4,2},{6,4},{1,7},{3,1},{5,3},{7,5},{8,14},{10,8},{12,... | collective-permute-start | bytes 417800 | tf_op jit(solution)/shard_map/ppermute | solution.py:200
  55.0 8.1 %collective-permute-start.2 = (f16[2,136,256]{2,1,0:T(8,128)(2,1)S(1)}, f16[2,136,256]{2,1,0:T(8,128)(2,1)S(1)}, u32[]{:S(2)}, u32[]{:S(2)}) collective-permute-start(f16[2,136,256]{2,1,0:T(8,128)(2,1)S(1)} %get-tuple-element.47), channel_id=1, source_target_pairs={{0,4},{2,6},{4,0},{6,2},{1,5},{3,7},{5,1},{7,3},{8,12},{10,14},{12... | collective-permute-start | bytes 417800 | tf_op jit(solution)/shard_map/ppermute | solution.py:200
  55.4 9.6 %collective-permute-start.1 = (f16[2,136,256]{2,1,0:T(8,128)(2,1)S(1)}, f16[2,136,256]{2,1,0:T(8,128)(2,1)S(1)}, u32[]{:S(2)}, u32[]{:S(2)}) collective-permute-start(f16[2,136,256]{2,1,0:T(8,128)(2,1)S(1)} %get-tuple-element.48), channel_id=1, source_target_pairs={{0,2},{2,4},{4,6},{6,0},{1,3},{3,5},{5,7},{7,1},{8,10},{10,12},{12... | collective-permute-start | bytes 417800 | tf_op jit(solution)/shard_map/ppermute | solution.py:200
  62.6 8.8 %collective-permute-start.4 = (f32[2048,256]{1,0:T(8,128)S(1)}, f32[2048,256]{1,0:T(8,128)S(1)}, u32[]{:S(2)}, u32[]{:S(2)}) collective-permute-start(f32[2048,256]{1,0:T(8,128)S(1)} %get-tuple-element.38), channel_id=1, source_target_pairs={{0,8},{8,0},{1,9},{9,1},{2,10},{10,2},{3,11},{11,3},{4,12},{12,4},... | collective-permute-start | bytes 6291464 | tf_op jit(solution)/shard_map/ppermute | solution.py:191
  65.1 6.7 %collective-permute-start.5 = (f32[128,256]{1,0:T(8,128)S(1)}, f32[128,256]{1,0:T(8,128)S(1)}, u32[]{:S(2)}, u32[]{:S(2)}) collective-permute-start(f32[128,256]{1,0:T(8,128)S(1)} %slice_bitcast_fusion.6), channel_id=1, source_target_pairs={{0,1},{1,0},{2,3},{3,2},{4,5},{5,4},{6,7},{7,6},{8,9},{9,8},{10,11... | collective-permute-start | bytes 393224 | tf_op jit(solution)/shard_map/ppermute | solution.py:214
